TPU v7x, 32 devices: a whole 2x2x4 slice. The times are simulated.
32 devices in a mesh: rep: 8 (over z, y), shard: 4 (over x, core).
Axes of the slice: x: 2, y: 2, z: 4, core: 2. Of those that a mesh axis runs over, the one named last changes fastest.
Arguments:
- tokens: bfloat16 [64, 384, 768], P(('rep', 'shard')), may hold values from -6 to 6
- ln1_gain: bfloat16 [768], P('shard'), may hold values from 0.099609375 to 1.8984375
- ln1_bias: bfloat16 [768], P('shard'), may hold values from -4 to 4
- qkv_weight: bfloat16 [768, 2304], P('shard'), may hold values from -0.21875 to 0.21875
- query_bias: bfloat16 [768], P('shard'), may hold values from -6 to 6
- value_bias: bfloat16 [768], P('shard'), may hold values from -6 to 6
- out_weight: bfloat16 [768, 768], P('shard'), may hold values from -0.625 to 0.625
- out_bias: bfloat16 [768], P('shard'), may hold values from -6 to 6
- ln2_gain: bfloat16 [768], P('shard'), may hold values from 0.099609375 to 1.8984375
- ln2_bias: bfloat16 [768], P('shard'), may hold values from -4 to 4
- fc1_weight: bfloat16 [768, 3072], P('shard'), may hold values from -0.21875 to 0.21875
- fc1_bias: bfloat16 [3072], P('shard'), may hold values from -6 to 6
- fc2_weight: bfloat16 [3072, 768], P('shard'), may hold values from -0.21875 to 0.21875
- fc2_bias: bfloat16 [768], P('shard'), may hold values from -6 to 6
- cotangent: bfloat16 [64, 384, 768], P(('rep', 'shard')), may hold values from -6 to 6
Outputs:
- output: bfloat16 [64, 384, 768], P(('rep', 'shard'))
- in_grad: bfloat16 [64, 384, 768], P(('rep', 'shard'))
- grad_ln1_gain: float32 [768], P('shard')
- grad_ln1_bias: float32 [768], P('shard')
- grad_qkv_weight: float32 [768, 2304], P('shard')
- grad_query_bias: float32 [768], P('shard')
- grad_value_bias: float32 [768], P('shard')
- grad_out_weight: float32 [768, 768], P('shard')
- grad_out_bias: float32 [768], P('shard')
- grad_ln2_gain: float32 [768], P('shard')
- grad_ln2_bias: float32 [768], P('shard')
- grad_fc1_weight: float32 [768, 3072], P('shard')
- grad_fc1_bias: float32 [3072], P('shard')
- grad_fc2_weight: float32 [3072, 768], P('shard')
- grad_fc2_bias: float32 [768], P('shard')
All inputs are finite; a program needn't handle non-finite values.
Results may differ from a plain program's by a relative error of at most 0.017.
Values may be sent and summed in bfloat16 or wider, within the bound.
No kernel may reach another device: no remote copies, remote signals or barrier semaphores. Data moves between devices by JAX's collectives and lax.ppermute only.
A program may use at most 192 MiB of HBM per device.

v0:
```python
from functools import partial
import math

import jax
import jax.numpy as jnp
from jax import lax
from jax.sharding import PartitionSpec as P

HEAD = 64


EPSILON = 1e-05


def normalize(values, scaling, offset):
    average = jnp.mean(values, axis=-1, keepdims=True)
    centred = values - average
    inverse = lax.rsqrt(jnp.mean(centred * centred, axis=-1, keepdims=True) + EPSILON)
    whitened = centred * inverse
    return (whitened * scaling + offset, whitened, inverse)


def norm_backward(incoming, whitened, inverse, scaling):
    scaled = incoming * scaling
    inner = (
        scaled
        - jnp.mean(scaled, axis=-1, keepdims=True)
        - whitened * jnp.mean(scaled * whitened, axis=-1, keepdims=True)
    )
    return (inner * inverse, jnp.sum(incoming * whitened, axis=0), jnp.sum(incoming, axis=0))


def matmul_plain(left, right):
    return jnp.dot(left, right, preferred_element_type=jnp.float32)


def matmul_left(left, right):
    return lax.dot_general(
        left, right, (((0,), (0,)), ((), ())), preferred_element_type=jnp.float32
    )


def matmul_right(left, right):
    return lax.dot_general(
        left, right, (((1,), (1,)), ((), ())), preferred_element_type=jnp.float32
    )


def causal_mask(length):
    return jnp.arange(length)[:, None] >= jnp.arange(length)[None, :]


def attention_forward(query, keys, values, factor):
    scores = jnp.einsum("sqhd,skhd->shqk", query, keys, preferred_element_type=jnp.float32) * factor
    masked = jnp.where(causal_mask(query.shape[1]), scores, -1e30)
    highest = jnp.max(masked, axis=-1, keepdims=True)
    expo = jnp.exp(masked - highest)
    totals = jnp.sum(expo, axis=-1, keepdims=True)
    probs = (expo / totals).astype(jnp.bfloat16)
    mixed = jnp.einsum("shqk,skhd->sqhd", probs, values, preferred_element_type=jnp.float32)
    return (mixed, highest + jnp.log(totals))


def attention_backward(query, keys, values, logsum, grad_mixed, factor):
    scores = jnp.einsum("sqhd,skhd->shqk", query, keys, preferred_element_type=jnp.float32) * factor
    probs = jnp.where(causal_mask(query.shape[1]), jnp.exp(scores - logsum), 0.0)
    grad_probs = jnp.einsum(
        "sqhd,skhd->shqk", grad_mixed, values, preferred_element_type=jnp.float32
    )
    grad_values = jnp.einsum(
        "shqk,sqhd->skhd",
        probs.astype(jnp.bfloat16),
        grad_mixed,
        preferred_element_type=jnp.float32,
    )
    inner = jnp.sum(probs * grad_probs, axis=-1, keepdims=True)
    grad_scores = (probs * (grad_probs - inner)).astype(jnp.bfloat16)
    grad_query = (
        jnp.einsum("shqk,skhd->sqhd", grad_scores, keys, preferred_element_type=jnp.float32)
        * factor
    )
    grad_keys = (
        jnp.einsum("shqk,sqhd->skhd", grad_scores, query, preferred_element_type=jnp.float32)
        * factor
    )
    return (
        grad_query.astype(jnp.bfloat16),
        grad_keys.astype(jnp.bfloat16),
        grad_values.astype(jnp.bfloat16),
    )


def on_device(
    tokens,
    ln1_gain,
    ln1_bias,
    qkv_weight,
    query_bias,
    value_bias,
    out_weight,
    out_bias,
    ln2_gain,
    ln2_bias,
    fc1_weight,
    fc1_bias,
    fc2_weight,
    fc2_bias,
    cotangent,
):
    f32 = jnp.float32
    bf16 = jnp.bfloat16
    attn_full = (
        lax.all_gather(ln1_gain, "shard", axis=0, tiled=True),
        lax.all_gather(ln1_bias, "shard", axis=0, tiled=True),
        lax.all_gather(qkv_weight, "shard", axis=0, tiled=True),
        lax.all_gather(query_bias, "shard", axis=0, tiled=True),
        lax.all_gather(value_bias, "shard", axis=0, tiled=True),
        lax.all_gather(out_weight, "shard", axis=0, tiled=True),
        lax.all_gather(out_bias, "shard", axis=0, tiled=True),
    )
    mlp_full = (
        lax.all_gather(ln2_gain, "shard", axis=0, tiled=True),
        lax.all_gather(ln2_bias, "shard", axis=0, tiled=True),
        lax.all_gather(fc1_weight, "shard", axis=0, tiled=True),
        lax.all_gather(fc1_bias, "shard", axis=0, tiled=True),
        lax.all_gather(fc2_weight, "shard", axis=0, tiled=True),
        lax.all_gather(fc2_bias, "shard", axis=0, tiled=True),
    )
    gain_one, bias_one, qkv_full, qbias_full, vbias_full, out_full, obias_full = attn_full
    gain_two, bias_two, fc1_full, fc1b_full, fc2_full, fc2b_full = mlp_full
    seqs_here, length, width = tokens.shape
    rows = seqs_here * length
    heads = width // HEAD
    factor = 1.0 / math.sqrt(HEAD)
    shape4 = (seqs_here, length, heads, HEAD)
    inputs = tokens.reshape(rows, width).astype(f32)
    normed_one, whitened_one, inverse_one = normalize(
        inputs, gain_one.astype(f32), bias_one.astype(f32)
    )
    first = normed_one.astype(bf16)
    packed = matmul_plain(first, qkv_full)
    query = (packed[:, :width] + qbias_full.astype(f32)).astype(bf16).reshape(shape4)
    keys = packed[:, width : 2 * width].astype(bf16).reshape(shape4)
    values = (packed[:, 2 * width :] + vbias_full.astype(f32)).astype(bf16).reshape(shape4)
    mixed, logsum = attention_forward(query, keys, values, factor)
    heads_out = mixed.reshape(rows, width).astype(bf16)
    hidden = inputs + matmul_plain(heads_out, out_full) + obias_full.astype(f32)
    normed_two, whitened_two, inverse_two = normalize(
        hidden, gain_two.astype(f32), bias_two.astype(f32)
    )
    second = normed_two.astype(bf16)
    pre_act = matmul_plain(second, fc1_full) + fc1b_full.astype(f32)
    activated = jax.nn.gelu(pre_act, approximate=True).astype(bf16)
    result = hidden + matmul_plain(activated, fc2_full) + fc2b_full.astype(f32)
    output = result.astype(bf16).reshape(tokens.shape)
    upstream = cotangent.reshape(rows, width)
    upstream_f = upstream.astype(f32)
    grad_fc2w = matmul_left(activated, upstream)
    grad_fc2b = jnp.sum(upstream_f, axis=0)
    grad_act = matmul_right(upstream, mlp_full[4])
    ignored, gelu_pull = jax.vjp(partial(jax.nn.gelu, approximate=True), pre_act)
    grad_pre = gelu_pull(grad_act)[0].astype(bf16)
    grad_fc1w = matmul_left(second, grad_pre)
    grad_fc1b = jnp.sum(grad_pre.astype(f32), axis=0)
    grad_second = matmul_right(grad_pre, mlp_full[2])
    grad_norm_two, grad_gain_two, grad_bias_two = norm_backward(
        grad_second, whitened_two, inverse_two, mlp_full[0].astype(f32)
    )
    grad_hidden = upstream_f + grad_norm_two
    branch = grad_hidden.astype(bf16)
    grad_outw = matmul_left(heads_out, branch)
    grad_outb = jnp.sum(branch.astype(f32), axis=0)
    grad_mixed = matmul_right(branch, attn_full[5]).astype(bf16).reshape(shape4)
    grad_query, grad_keys, grad_values = attention_backward(
        query, keys, values, logsum, grad_mixed, factor
    )
    grad_query = grad_query.reshape(rows, width)
    grad_values = grad_values.reshape(rows, width)
    grad_packed = jnp.concatenate([grad_query, grad_keys.reshape(rows, width), grad_values], axis=1)
    grad_qkvw = matmul_left(first, grad_packed)
    grad_qbias = jnp.sum(grad_query.astype(f32), axis=0)
    grad_vbias = jnp.sum(grad_values.astype(f32), axis=0)
    grad_first = matmul_right(grad_packed, attn_full[2])
    grad_norm_one, grad_gain_one, grad_bias_one = norm_backward(
        grad_first, whitened_one, inverse_one, attn_full[0].astype(f32)
    )
    in_grad = (grad_hidden + grad_norm_one).astype(bf16).reshape(tokens.shape)
    (
        owned_g1,
        owned_b1,
        owned_qkv,
        owned_qb,
        owned_vb,
        owned_ow,
        owned_ob,
        owned_g2,
        owned_b2,
        owned_w1,
        owned_c1,
        owned_w2,
        owned_c2,
    ) = (
        lax.psum_scatter(
            grad_gain_one.astype(jnp.bfloat16), "shard", scatter_dimension=0, tiled=True
        ).astype(jnp.float32),
        lax.psum_scatter(
            grad_bias_one.astype(jnp.bfloat16), "shard", scatter_dimension=0, tiled=True
        ).astype(jnp.float32),
        lax.psum_scatter(
            grad_qkvw.astype(jnp.bfloat16), "shard", scatter_dimension=0, tiled=True
        ).astype(jnp.float32),
        lax.psum_scatter(
            grad_qbias.astype(jnp.bfloat16), "shard", scatter_dimension=0, tiled=True
        ).astype(jnp.float32),
        lax.psum_scatter(
            grad_vbias.astype(jnp.bfloat16), "shard", scatter_dimension=0, tiled=True
        ).astype(jnp.float32),
        lax.psum_scatter(
            grad_outw.astype(jnp.bfloat16), "shard", scatter_dimension=0, tiled=True
        ).astype(jnp.float32),
        lax.psum_scatter(
            grad_outb.astype(jnp.bfloat16), "shard", scatter_dimension=0, tiled=True
        ).astype(jnp.float32),
        lax.psum_scatter(
            grad_gain_two.astype(jnp.bfloat16), "shard", scatter_dimension=0, tiled=True
        ).astype(jnp.float32),
        lax.psum_scatter(
            grad_bias_two.astype(jnp.bfloat16), "shard", scatter_dimension=0, tiled=True
        ).astype(jnp.float32),
        lax.psum_scatter(
            grad_fc1w.astype(jnp.bfloat16), "shard", scatter_dimension=0, tiled=True
        ).astype(jnp.float32),
        lax.psum_scatter(
            grad_fc1b.astype(jnp.bfloat16), "shard", scatter_dimension=0, tiled=True
        ).astype(jnp.float32),
        lax.psum_scatter(
            grad_fc2w.astype(jnp.bfloat16), "shard", scatter_dimension=0, tiled=True
        ).astype(jnp.float32),
        lax.psum_scatter(
            grad_fc2b.astype(jnp.bfloat16), "shard", scatter_dimension=0, tiled=True
        ).astype(jnp.float32),
    )
    summed = lax.psum(
        (
            owned_g1,
            owned_b1,
            owned_qkv,
            owned_qb,
            owned_vb,
            owned_ow,
            owned_ob,
            owned_g2,
            owned_b2,
            owned_w1,
            owned_c1,
            owned_w2,
            owned_c2,
        ),
        "rep",
    )
    return (
        output,
        in_grad,
        summed[0],
        summed[1],
        summed[2],
        summed[3],
        summed[4],
        summed[5],
        summed[6],
        summed[7],
        summed[8],
        summed[9],
        summed[10],
        summed[11],
        summed[12],
    )


def solution(mesh):
    return jax.shard_map(
        on_device,
        mesh=mesh,
        in_specs=(
            P(("rep", "shard"), None, None),
            P("shard"),
            P("shard"),
            P("shard", None),
            P("shard"),
            P("shard"),
            P("shard", None),
            P("shard"),
            P("shard"),
            P("shard"),
            P("shard", None),
            P("shard"),
            P("shard", None),
            P("shard"),
            P(("rep", "shard"), None, None),
        ),
        out_specs=(
            P(("rep", "shard"), None, None),
            P(("rep", "shard"), None, None),
            P("shard"),
            P("shard"),
            P("shard", None),
            P("shard"),
            P("shard"),
            P("shard", None),
            P("shard"),
            P("shard"),
            P("shard"),
            P("shard", None),
            P("shard"),
            P("shard", None),
            P("shard"),
        ),
        check_vma=False,
    )
```

profile of v0, /device:TPU:0, one launch (start us, length us, event | category | flops | bytes accessed | tf_op | source)
XLA Modules:
  0.0 656.2 jit_solution(482723273535011183)
XLA Ops:
  13.8 13.2 %all-reduce.19 = (bf16[768]{0:T(1024)(128)(2,1)S(1)}, bf16[768]{0:T(1024)(128)(2,1)S(1)}, bf16[768]{0:T(1024)(128)(2,1)S(1)}, bf16[768]{0:T(1024)(128)(2,1)S(1)}...) all-reduce(bf16[768]{0:T(1024)(128)(2,1)S(1)} %dynamic-update-slice, ...), channel_id=1, replica_groups=mesh['rep'=8,'shard'=4] {'shard'}, use_global_device_ids=true, to_apply=%add.1 | all-reduce | flops 5376 | bytes 21504
  30.7 5.2 all-gather
  36.5 6.8 %all-gather.6.cloned.1.call-done = bf16[768,2304]{1,0:T(8,128)(2,1)} async-done(((bf16[192,2304]{1,0:T(8,128)(2,1)}), bf16[768,2304]{1,0:T(8,128)(2,1)}) %all-gather.6.cloned.1.call-update) | async-done | bytes 3538960 | tf_op jit(solution)/shard_map/all_gather | solution.py:115
  43.3 4.9 fusion.64
  64.8 7.9 %select_reduce_fusion = (f32[2,12,384]{2,1,0:T(8,128)S(1)}, f32[2,12,384,384]{2,3,1,0:T(8,128)}) fusion(pred[384,384]{0,1:T(8,128)(4,1)} %iota_compare_fusion, bf16[2,384,12,64]{1,0,3,2:T(2,128)(2,1)S(1)} %reshape.149, bf16[2,384,12,64]{1,0,3,2:T(2,128)(2,1)S(1)} %reshape.148), kind=kOutput, calls=%fused_computation.7 | convolution fusion | flops 463592448 | bytes 16699392 | tf_op jit(solution)/shard_map/sqhd,skhd->shqk/dot_general | solution.py:54
  72.7 8.3 %fusion = f32[2,12,384]{2,1,0:T(8,128)S(1)} fusion(f32[2,12,384,384]{2,3,1,0:T(8,128)} %get-tuple-element.62, f32[2,12,384]{2,1,0:T(8,128)S(1)} %get-tuple-element.61, pred[384,384]{0,1:T(8,128)(4,1)S(1)} %copy-done.7), kind=kLoop, calls=%fused_computation.8 | loop fusion | flops 14146560 | bytes 14376960 | tf_op jit(solution)/shard_map/reduce_sum | solution.py:58
  81.1 9.3 %fusion.35 = bf16[2,384,12,64]{1,3,2,0:T(8,128)(2,1)S(1)} fusion(f32[2,12,384,384]{2,3,1,0:T(8,128)} %get-tuple-element.62, f32[2,12,384]{2,1,0:T(8,128)S(1)} %fusion, f32[2,12,384]{2,1,0:T(8,128)S(1)} %get-tuple-element.61, pred[384,384]{0,1:T(8,128)(4,1)S(1)} %copy-done.7, bf16[2,384,12,64]{1,0,3,2:T(2,128)(2,1)S(1)} %copy-done.11), kind=kOutput, calls=%fused_computation.64 | convolution fusion | flops 471269376 | bytes 16736256 | tf_op jit(solution)/shard_map/shqk,skhd->sqhd/dot_general | solution.py:60
  101.4 22.0 %fusion.57 = f32[768,3072]{1,0:T(8,128)} fusion(bf16[768,3072]{1,0:T(8,128)(2,1)} %all-gather.10.cloned.1.call-done, f32[768,768]{1,0:T(8,128)} %copy-done.3, f32[768]{0:T(1024)} %convert_element_type.197, f32[768]{0:T(1024)} %convert_element_type.196, f32[768]{0:T(1024)} %add_rsqrt_fusion, f32[768]{0:T(1024)S(1)} %broadcast_multiply_fusion.4), kind=kOutput, calls=%fused_computation.107 | convolution fusion | flops 3626827776 | bytes 16527360 | tf_op jit(solution)/shard_map/dot_general | solution.py:34
  123.4 16.9 %all-gather.12.cloned.1.call-done = bf16[3072,768]{1,0:T(8,128)(2,1)} async-done(((bf16[768,768]{1,0:T(8,128)(2,1)}), bf16[3072,768]{1,0:T(8,128)(2,1)}) %all-gather.12.cloned.1.call-update) | async-done | bytes 4718608 | tf_op jit(solution)/shard_map/all_gather | solution.py:126
  140.3 13.4 %fusion.58 = (bf16[3072]{0:T(1024)(128)(2,1)}, bf16[768,3072]{1,0:T(8,128)(2,1)S(1)}) fusion(f32[768,3072]{1,0:T(8,128)} %fusion.57, f32[3072]{0:T(1024)} %bitcast.111, bf16[768,768]{1,0:T(8,128)(2,1)} %bitcast.106, bf16[3072,768]{1,0:T(8,128)(2,1)} %all-gather.12.cloned.1.call-done), kind=kOutput, calls=%fused_computation.108 | convolution fusion | flops 3675780096 | bytes 20072448 | tf_op jit(solution)/shard_map/dot_general | solution.py:44
  153.8 4.9 multiply_reduce_fusion.1
  174.1 15.3 %multiply_reduce_fusion = (f32[2,12,384]{2,1,0:T(8,128)S(1)}, f32[2,12,384,384]{2,3,1,0:T(8,128)}) fusion(f32[2,12,384,384]{2,3,1,0:T(8,128)} %get-tuple-element.62, f32[2,12,384]{2,1,0:T(8,128)} %log_add_fusion, pred[384,384]{0,1:T(8,128)(4,1)} %iota_compare_fusion, bf16[2,384,12,64]{1,0,3,2:T(2,128)(2,1)} %reshape.147, bf16[2,384,12,64]{1,0,3,2:T(2,128)(2,1)} %reshape.152), kind=kOutput, calls=%fused_computation.1 | convolution fusion | flops 470670336 | bytes 30892032 | tf_op jit(solution)/shard_map/sqhd,skhd->shqk/dot_general | solution.py:67
  189.5 14.3 %multiply_convert_fusion = bf16[2,12,384,384]{2,3,1,0:T(8,128)(2,1)} fusion(f32[2,12,384,384]{2,3,1,0:T(8,128)} %get-tuple-element.67, f32[2,12,384,384]{2,3,1,0:T(8,128)} %get-tuple-element.62, f32[2,12,384]{2,1,0:T(8,128)S(1)} %get-tuple-element.66, f32[2,12,384]{2,1,0:T(8,128)S(1)} %copy-done.18, pred[384,384]{0,1:T(8,128)(4,1)S(1)} %copy-done.8), kind=kLoop, calls=%fused_computation | loop fusion | flops 21233664 | bytes 35610624 | tf_op jit(solution)/shard_map/convert_element_type | solution.py:77
  203.8 4.8 fusion.63
  211.3 5.8 fusion.40
  224.1 4.5 convolution_convert_fusion
  230.2 8.4 %convolution_convert_fusion.2 = bf16[768,3072]{1,0:T(8,128)(2,1)} fusion(bf16[768,3072]{1,0:T(8,128)(2,1)} %copy-done.50, f32[768,768]{1,0:T(8,128)S(1)} %copy-done.5, f32[768]{0:T(1024)} %convert_element_type.197, f32[768]{0:T(1024)} %convert_element_type.196, f32[768]{0:T(1024)} %add_rsqrt_fusion, f32[768]{0:T(1024)S(1)} %broadcast_multiply_fusion.4), kind=kOutput, calls=%fused_computation.23 | convolution fusion | flops 3629187072 | bytes 11808768 | tf_op jit(solution)/shard_map/dot_general | solution.py:38
  240.0 11.6 %convolution_convert_fusion.1 = bf16[3072,768]{1,0:T(8,128)(2,1)} fusion(bf16[768,768]{1,0:T(8,128)(2,1)S(1)} %bitcast.107, f32[768,3072]{1,0:T(8,128)} %fusion.57, f32[3072]{0:T(1024)S(1)} %bitcast.112), kind=kOutput, calls=%fused_computation.22 | convolution fusion | flops 3649830912 | bytes 15347712 | tf_op jit(solution)/shard_map/dot_general | solution.py:38
  254.8 8.6 %fusion.29 = (bf16[768]{0:T(1024)(128)(2,1)}, f32[768]{0:T(1024)}, f32[768]{0:T(1024)}, bf16[768]{0:T(1024)(128)(2,1)}, f32[768,768]{1,0:T(8,128)}) fusion(bf16[2,384,768]{2,1,0:T(8,128)(2,1)S(1)} %copy-done, f32[768]{0:T(1024)S(1)} %rsqrt.20, f32[768]{0:T(1024)S(1)} %div.35, f32[768]{0:T(1024)S(1)} %convert_element_type.184, ...), kind=kOutput, calls=%fused_computation.47 | convolution fusion | flops 2723804160 | bytes 10635264 | tf_op jit(solution)/shard_map/dot_general | solution.py:44
  263.4 11.8 %all-reduce.18 = (bf16[768]{0:T(1024)(128)(2,1)}, bf16[768]{0:T(1024)(128)(2,1)}, bf16[768]{0:T(1024)(128)(2,1)}, bf16[768]{0:T(1024)(128)(2,1)}, bf16[768]{0:T(...) all-reduce(bf16[768]{0:T(1024)(128)(2,1)} %copy-done.28, ...), channel_id=1, replica_groups=mesh['rep'=8,'shard'=4] {'shard'}, use_global_device_ids=true, to_apply=%add.7 | all-reduce | flops 9984 | bytes 39936
  291.9 12.0 %add_convert_fusion = bf16[768,768]{1,0:T(8,128)(2,1)} fusion(f32[768,768]{1,0:T(8,128)S(1)} %copy-done.6, bf16[3072,768]{1,0:T(8,128)(2,1)} %all-gather.12.cloned.1.call-done, f32[768]{0:T(1024)S(1)} %convert_element_type.201, f32[768,3072]{1,0:T(8,128)} %fusion.57, f32[3072]{0:T(1024)S(1)} %bitcast.113), kind=kOutput, calls=%fused_computation.54 | convolution fusion | flops 3649241088 | bytes 17710080 | tf_op jit(solution)/shard_map/dot_general | solution.py:34
  303.9 15.5 %reduce-scatter.9.cloned.1.call-done = bf16[192,3072]{1,0:T(8,128)(2,1)} async-done(((bf16[768,3072]{1,0:T(8,128)(2,1)}), bf16[192,3072]{1,0:T(8,128)(2,1)}) %reduce-scatter.9.cloned.1.call-update) | async-done | bytes 1179664 | tf_op jit(solution)/shard_map/reduce_scatter | solution.py:230
  319.4 50.6 %reduce-scatter.11.cloned.1.call-done = bf16[768,768]{1,0:T(8,128)(2,1)} async-done(((bf16[3072,768]{1,0:T(8,128)(2,1)}), bf16[768,768]{1,0:T(8,128)(2,1)}) %reduce-scatter.11.cloned.1.call-update) | async-done | bytes 1179664 | tf_op jit(solution)/shard_map/reduce_scatter | solution.py:236
  370.0 279.1 %all-reduce.21 = (f32[192]{0:T(256)}, f32[192]{0:T(256)}, f32[192,2304]{1,0:T(8,128)}, f32[192]{0:T(256)}, f32[192]{0:T(256)}, /*index=5*/f32[192,768]{1,0:T(8,1...) all-reduce(f32[192]{0:T(256)S(1)} %copy-done.38, ...), channel_id=1, replica_groups=mesh['rep'=8,'shard'=4] {'rep'}, use_global_device_ids=true, to_apply=%region_13.14 | all-reduce | flops 1771776 | bytes 10635264 | tf_op jit(solution)/shard_map/psum | solution.py:243
  (217 shorter events, 84.1 us)
Async XLA Ops:
  7.2 36.1 %all-gather.6.cloned.1.call-start = ((), (), s32[]{:S(2)}) async-start(), calls=%async_computation.4 | async-start | bytes 4423680 | tf_op jit(solution)/shard_map/all_gather | solution.py:115
  7.9 84.9 %all-gather.8.cloned.1.call-start = ((), (), s32[]{:S(2)}) async-start(), calls=%async_computation.5 | async-start | bytes 1474560 | tf_op jit(solution)/shard_map/all_gather | solution.py:118
  8.8 92.6 %all-gather.10.cloned.1.call-start = ((), (), s32[]{:S(2)}) async-start(), calls=%async_computation.6 | async-start | bytes 5898240 | tf_op jit(solution)/shard_map/all_gather | solution.py:124
  9.5 130.8 %all-gather.12.cloned.1.call-start = ((), (), s32[]{:S(2)}) async-start(), calls=%async_computation.7 | async-start | bytes 5898240 | tf_op jit(solution)/shard_map/all_gather | solution.py:126
  10.1 293.8 %reduce-scatter.7.cloned.1.call-start = ((), (), s32[]{:S(2)}) async-start(), calls=%async_computation.9 | async-start | bytes 1474560 | tf_op jit(solution)/shard_map/reduce_scatter | solution.py:218
  10.1 20.5 %copy-start.40 = (bf16[768]{0:T(1024)(128)(2,1)S(1)}, bf16[768]{0:T(1024)(128)(2,1)}, u32[]{:S(2)}) copy-start(bf16[768]{0:T(1024)(128)(2,1)} %param.26) | copy-start | bytes 4612
  27.5 15.8 %copy-start.13 = (bf16[768,768]{1,0:T(8,128)(2,1)}, bf16[768,768]{1,0:T(8,128)(2,1)S(1)}, u32[]{:S(2)}) copy-start(bf16[768,768]{1,0:T(8,128)(2,1)S(1)} %fusion.23) | copy-start | bytes 3538948
  174.1 129.9 %reduce-scatter.5.cloned.1.call-start = ((), (), s32[]{:S(2)}) async-start(), calls=%async_computation.8 | async-start | bytes 4423680 | tf_op jit(solution)/shard_map/reduce_scatter | solution.py:209
  174.1 15.3 %copy-start.8 = (pred[384,384]{0,1:T(8,128)(4,1)S(1)}, pred[384,384]{0,1:T(8,128)(4,1)}, u32[]{:S(2)}) copy-start(pred[384,384]{0,1:T(8,128)(4,1)} %iota_compare_fusion) | copy-start | bytes 442372
  174.1 15.3 %copy-start.18 = (f32[2,12,384]{2,1,0:T(8,128)S(1)}, f32[2,12,384]{2,1,0:T(8,128)}, u32[]{:S(2)}) copy-start(f32[2,12,384]{2,1,0:T(8,128)} %log_add_fusion) | copy-start | bytes 110596
  174.1 29.6 %slice-start = ((s8[14155776]{0:T(1024)(128)(4,1)}), s8[4194304]{0:T(1024)(128)(4,1)S(1)}, s32[]{:S(2)}) async-start(s8[14155776]{0:T(1024)(128)(4,1)} %bitcast.95), calls=%async_computation.12 | async-start | bytes 8388608
  174.1 29.6 %slice-start.1 = ((s8[14155776]{0:T(1024)(128)(4,1)}), s8[4194304]{0:T(1024)(128)(4,1)S(1)}, s32[]{:S(2)}) async-start(s8[14155776]{0:T(1024)(128)(4,1)} %bitcast.95), calls=%async_computation.13 | async-start | bytes 8388608
  189.4 14.3 %slice-start.3 = ((s8[14155776]{0:T(1024)(128)(4,1)}), s8[1572864]{0:T(1024)(128)(4,1)S(1)}, s32[]{:S(2)}) async-start(s8[14155776]{0:T(1024)(128)(4,1)} %bitcast.95), calls=%async_computation.15 | async-start | bytes 3145728
  228.6 90.8 %reduce-scatter.9.cloned.1.call-start = ((), (), s32[]{:S(2)}) async-start(), calls=%async_computation.10 | async-start | bytes 5898240 | tf_op jit(solution)/shard_map/reduce_scatter | solution.py:230
  238.7 131.3 %reduce-scatter.11.cloned.1.call-start = ((), (), s32[]{:S(2)}) async-start(), calls=%async_computation.11 | async-start | bytes 5898240 | tf_op jit(solution)/shard_map/reduce_scatter | solution.py:236
  254.8 33.8 %copy-start.2 = (f32[768,768]{1,0:T(8,128)S(1)}, f32[768,768]{1,0:T(8,128)}, u32[]{:S(2)}) copy-start(f32[768,768]{1,0:T(8,128)} %copy-done.1) | copy-start | bytes 7077892
  291.8 78.2 %copy-start.31 = (f32[192]{0:T(256)S(1)}, f32[192]{0:T(256)}, u32[]{:S(2)}) copy-start(f32[192]{0:T(256)} %dynamic-slice_convert_fusion.1) | copy-start | bytes 2308
  291.8 78.2 %copy-start.32 = (f32[192]{0:T(256)S(1)}, f32[192]{0:T(256)}, u32[]{:S(2)}) copy-start(f32[192]{0:T(256)} %dynamic-slice_convert_fusion.2) | copy-start | bytes 2308
  291.8 78.2 %copy-start.33 = (f32[192]{0:T(256)S(1)}, f32[192]{0:T(256)}, u32[]{:S(2)}) copy-start(f32[192]{0:T(256)} %dynamic-slice_convert_fusion.3) | copy-start | bytes 2308
  291.8 78.2 %copy-start.34 = (f32[192]{0:T(256)S(1)}, f32[192]{0:T(256)}, u32[]{:S(2)}) copy-start(f32[192]{0:T(256)} %dynamic-slice_convert_fusion.4) | copy-start | bytes 2308
  291.8 78.2 %copy-start.35 = (f32[192]{0:T(256)S(1)}, f32[192]{0:T(256)}, u32[]{:S(2)}) copy-start(f32[192]{0:T(256)} %dynamic-slice_convert_fusion.5) | copy-start | bytes 2308
  291.8 78.2 %copy-start.36 = (f32[192]{0:T(256)S(1)}, f32[192]{0:T(256)}, u32[]{:S(2)}) copy-start(f32[192]{0:T(256)} %dynamic-slice_convert_fusion.6) | copy-start | bytes 2308
  291.8 78.2 %copy-start.37 = (f32[192]{0:T(256)S(1)}, f32[192]{0:T(256)}, u32[]{:S(2)}) copy-start(f32[192]{0:T(256)} %dynamic-slice_convert_fusion.7) | copy-start | bytes 2308
  291.9 78.2 %copy-start.38 = (f32[192]{0:T(256)S(1)}, f32[192]{0:T(256)}, u32[]{:S(2)}) copy-start(f32[192]{0:T(256)} %dynamic-slice_convert_fusion.8) | copy-start | bytes 2308
  (41 other events, 210.3 us)
Sparse Core Ops, SparseCore 0:
  9.6 33.6 all-gather.5
  44.8 17.4 all-gather.7
  63.9 37.4 all-gather.9
  102.8 37.4 all-gather.11
  174.2 25.7 reduce-scatter.6
  228.7 40.2 reduce-scatter.4
  271.6 47.8 reduce-scatter.8
  322.1 47.8 reduce-scatter.10
where the time goes:
time: 665 us; the launch traced here: 656 us
  blocking collectives  309 us (46%)
  matrix products  145 us (22%)
  waiting for transfers between devices  94.9 us (14%)
  other arithmetic  49 us (7%)
  local copies, waits for them, and re-layouts  40.9 us (6%)
  between operations  17 us (3%)
    psum x1, blocking collectives, on_device(): lax.psum((owned_g1, owned_b1, owned_qkv, owned_qb, owned_vb, owned_ow, ow...  279 us
    reduce_scatter x1, waiting for transfers between devices, on_device(): lax.psum_scatter(grad_fc2w.astype(jnp.bfloat16), 'shard', scatter_dimensi...  50.6 us
    dot_general x4, matrix products, matmul_plain(): return jnp.dot(left, right, preferred_element_type=jnp.float32)  41.9 us
    dot_general x4, matrix products, matmul_right(): lax.dot_general(left, right, (((1,), (1,)), ((), ())), preferred_element_...  31.1 us
    dot_general x4, matrix products, matmul_left(): lax.dot_general(left, right, (((0,), (0,)), ((), ())), preferred_element_...  26.8 us
    unnamed x2, blocking collectives  25 us
    all_gather x1, waiting for transfers between devices, on_device(): lax.all_gather(fc2_weight, 'shard', axis=0, tiled=True)  16.9 us
    reduce_scatter x1, waiting for transfers between devices, on_device(): lax.psum_scatter(grad_fc1w.astype(jnp.bfloat16), 'shard', scatter_dimensi...  15.5 us
  transfers between devices with their start and end apart: 8, of which 5 were waited for; matrix products, arithmetic and copies ran while one was open for 30% of the time, Pallas kernels for 0%

commit v1 on v0

v1 whole, which is shorter than its diff:
```python
from functools import partial
import math

import jax
import jax.numpy as jnp
from jax import lax
from jax.experimental import pallas as pl
from jax.experimental.pallas import tpu as pltpu
from jax.sharding import PartitionSpec as P

HEAD = 64
EPSILON = 1e-05
F32 = jnp.float32
BF16 = jnp.bfloat16
LIMIT = 56 * 1024 * 1024
TANH_SCALE = math.sqrt(2.0 / math.pi)


def dot_nn(left, right):
    return jnp.dot(left, right, preferred_element_type=F32)


def dot_nt(left, right):
    return lax.dot_general(left, right, (((1,), (1,)), ((), ())), preferred_element_type=F32)


def dot_tn(left, right):
    return lax.dot_general(left, right, (((0,), (0,)), ((), ())), preferred_element_type=F32)


def whole(shape):
    return pl.BlockSpec(shape, lambda *_: (0,) * len(shape))


HBM = pl.BlockSpec(memory_space=pl.ANY)
ROW_XOR = (0, 2, 1, 3)


def weight_copies(info, pieces, target, sems):
    me, half = info[0], info[1]
    block = pieces[0].shape[0]
    part = block // 2
    rows = (
        me * block,
        (me ^ 1) * block,
        (me ^ 2) * block + half * part,
        (me ^ 2) * block + (1 - half) * part,
        (me ^ 3) * block + half * part,
        (me ^ 3) * block + (1 - half) * part,
    )
    copies = []
    for index, (piece, row) in enumerate(zip(pieces, rows)):
        size = piece.shape[0]
        row = pl.multiple_of(row, 16)
        copies.append(
            pltpu.make_async_copy(piece, target.at[pl.ds(row, size), :], sems.at[index])
        )
    return copies


def norm_parts(values):
    average = jnp.mean(values, axis=-1, keepdims=True)
    centred = values - average
    inverse = lax.rsqrt(jnp.mean(centred * centred, axis=-1, keepdims=True) + EPSILON)
    return centred * inverse, inverse


def triangle(block):
    return lax.broadcasted_iota(jnp.int32, (block, block), 0) <= lax.broadcasted_iota(
        jnp.int32, (block, block), 1
    )


def attend_kernel(length, info, tok, vec, *refs):
    pieces, (first, packed, mixed, logsum), (weight, sems) = refs[:6], refs[6:10], refs[10:]
    rows, width = tok.shape
    copies = weight_copies(info, pieces, weight, sems)
    for copy in copies:
        copy.start()

    def norm_step(i, _):
        at = pl.ds(pl.multiple_of(i * 128, 128), 128)
        white, _inverse = norm_parts(tok[at, :].astype(F32))
        first[at, :] = (white * vec[0:1, :] + vec[1:2, :]).astype(BF16)
        return 0

    lax.fori_loop(0, rows // 128, norm_step, 0)
    for copy in copies:
        copy.wait()

    for part in range(3):
        def project(i, _, part=part):
            at = pl.ds(pl.multiple_of(i * 256, 256), 256)
            to = pl.ds(pl.multiple_of(part * width + i * 256, 256), 256)
            value = dot_nn(first[...], weight[:, to])
            if part == 0:
                value = (value + vec[2:3, at]).astype(BF16) * jnp.asarray(HEAD**-0.5, BF16)
            elif part == 2:
                value = (value + vec[3:4, at]).astype(BF16)
            else:
                value = value.astype(BF16)
            packed[:, to] = value
            return 0

        lax.fori_loop(0, width // 256, project, 0)

    pairs = width // 128
    blocks = length // 128
    keep = triangle(128)

    def pair_step(it, _):
        base = (it // pairs) * length
        column = (it % pairs) * 128
        at = pl.ds(pl.multiple_of(base, 128), length)
        query = packed[at, pl.ds(pl.multiple_of(column, 128), 128)]
        key = packed[at, pl.ds(pl.multiple_of(width + column, 128), 128)]
        value = packed[at, pl.ds(pl.multiple_of(2 * width + column, 128), 128)]
        lane = lax.broadcasted_iota(jnp.int32, query.shape, 1)
        halves = []
        for head in range(2):
            masked = jnp.where((lane < HEAD) == (head == 0), query, jnp.zeros_like(query))
            scores = [
                dot_nt(key[kb * 128 : (kb + 1) * 128], masked[kb * 128 :]) for kb in range(blocks)
            ]
            outs = []
            for qb in range(blocks):
                tiles = [
                    scores[kb][:, (qb - kb) * 128 : (qb - kb + 1) * 128] for kb in range(qb + 1)
                ]
                tiles[qb] = jnp.where(keep, tiles[qb], -1e30)
                highest = tiles[0]
                for tile in tiles[1:]:
                    highest = jnp.maximum(highest, tile)
                highest = jnp.max(highest, axis=0, keepdims=True)
                expo = [jnp.exp(tile - highest) for tile in tiles]
                total = expo[0]
                for tile in expo[1:]:
                    total = total + tile
                total = jnp.sum(total, axis=0, keepdims=True)
                scale = 1.0 / total
                probs = jnp.concatenate([(tile * scale).astype(BF16) for tile in expo], axis=0)
                outs.append(dot_tn(value[: (qb + 1) * 128], probs))
                logsum[it * 2 + head, 0:1, qb * 128 : (qb + 1) * 128] = highest + jnp.log(total)
            halves.append(outs)
        for qb in range(blocks):
            both = jnp.concatenate([halves[0][qb][:HEAD], halves[1][qb][HEAD:]], axis=0)
            mixed[
                pl.ds(pl.multiple_of(base + qb * 128, 128), 128),
                pl.ds(pl.multiple_of(column, 128), 128),
            ] = both.T.astype(BF16)
        return 0

    lax.fori_loop(0, (rows // length) * pairs, pair_step, 0)


def attend(info, tok, vec, pieces, length):
    rows, width = tok.shape
    groups = (rows // length) * (width // HEAD)
    return pl.pallas_call(
        partial(attend_kernel, length),
        in_specs=[pl.BlockSpec(memory_space=pltpu.SMEM)]
        + [pl.BlockSpec(memory_space=pltpu.VMEM)] * 2
        + [HBM] * 6,
        out_specs=[pl.BlockSpec(memory_space=pltpu.VMEM)] * 4,
        out_shape=[
            jax.ShapeDtypeStruct((rows, width), BF16),
            jax.ShapeDtypeStruct((rows, 3 * width), BF16),
            jax.ShapeDtypeStruct((rows, width), BF16),
            jax.ShapeDtypeStruct((groups, 1, length), F32),
        ],
        scratch_shapes=[pltpu.VMEM((width, 3 * width), BF16), pltpu.SemaphoreType.DMA((6,))],
        compiler_params=pltpu.CompilerParams(vmem_limit_bytes=LIMIT),
        cost_estimate=pl.CostEstimate(
            flops=2 * rows * width * 3 * width * 3, bytes_accessed=12000000, transcendentals=0
        ),
        name="attend",
    )(info, tok, vec, *pieces)


def feed_kernel(info, mixed, tok, vec, bias, *refs):
    out_pieces, fc1_pieces = refs[:6], refs[6:12]
    hidden, second, act, slope = refs[12:16]
    out_w, fc1_w, sems = refs[16:]
    step = pl.program_id(0)
    rows, width = tok.shape
    chunk = act.shape[1]

    @pl.when(step == 0)
    def _():
        out_copies = weight_copies(info, out_pieces, out_w, sems.at[0])
        fc1_copies = weight_copies(info, fc1_pieces, fc1_w, sems.at[1])
        for copy in out_copies + fc1_copies:
            copy.start()
        for copy in out_copies:
            copy.wait()

        def norm_step(i, _):
            at = pl.ds(pl.multiple_of(i * 256, 256), 256)
            value = tok[at, :].astype(F32) + dot_nn(mixed[at, :], out_w[...]) + vec[4:5, :]
            hidden[at, :] = value
            white, _inverse = norm_parts(value)
            second[at, :] = (white * vec[5:6, :] + vec[6:7, :]).astype(BF16)
            return 0

        lax.fori_loop(0, rows // 256, norm_step, 0)
        for copy in fc1_copies:
            copy.wait()

    columns = pl.ds(pl.multiple_of(step * chunk, chunk), chunk)

    def gelu_step(i, _):
        at = pl.ds(pl.multiple_of(i * 256, 256), 256)
        u = dot_nn(second[at, :], fc1_w[:, columns]) + bias[...]
        square = u * u
        t = jnp.tanh(u * (TANH_SCALE + (TANH_SCALE * 0.044715) * square))
        left = 0.5 + 0.5 * t
        act[at, :] = (u * left).astype(BF16)
        inner = TANH_SCALE + (3 * TANH_SCALE * 0.044715) * square
        slope[at, :] = (left + u * (0.5 - 0.5 * t * t) * inner).astype(BF16)
        return 0

    lax.fori_loop(0, rows // 256, gelu_step, 0)


def feed(info, mixed, tok, vec, bias, out_pieces, fc1_pieces):
    rows, width = tok.shape
    ff = bias.shape[1]
    chunk = 512
    return pl.pallas_call(
        feed_kernel,
        grid=(ff // chunk,),
        in_specs=[
            pl.BlockSpec(memory_space=pltpu.SMEM),
            whole((rows, width)),
            whole((rows, width)),
            whole(vec.shape),
            pl.BlockSpec((1, chunk), lambda j: (0, j)),
        ]
        + [HBM] * 12,
        out_specs=[
            whole((rows, width)),
            whole((rows, width)),
            pl.BlockSpec((rows, chunk), lambda j: (0, j)),
            pl.BlockSpec((rows, chunk), lambda j: (0, j)),
        ],
        out_shape=[
            jax.ShapeDtypeStruct((rows, width), F32),
            jax.ShapeDtypeStruct((rows, width), BF16),
            jax.ShapeDtypeStruct((rows, ff), BF16),
            jax.ShapeDtypeStruct((rows, ff), BF16),
        ],
        scratch_shapes=[
            pltpu.VMEM((width, width), BF16),
            pltpu.VMEM((width, ff), BF16),
            pltpu.SemaphoreType.DMA((2, 6)),
        ],
        compiler_params=pltpu.CompilerParams(
            vmem_limit_bytes=LIMIT, dimension_semantics=("arbitrary",)
        ),
        cost_estimate=pl.CostEstimate(
            flops=2 * rows * width * (width + ff) * 2, bytes_accessed=20000000, transcendentals=0
        ),
        name="feed",
    )(info, mixed, tok, vec, bias, *out_pieces, *fc1_pieces)


def down_grad_kernel(info, act, dy, send, keep, sums):
    step = pl.program_id(0)

    @pl.when(step == 0)
    def _():
        sums[...] = jnp.sum(dy[...].astype(F32), axis=0, keepdims=True)

    grad = dot_tn(act[...], dy[...]).astype(BF16)

    @pl.when(step < 6)
    def _():
        send[0] = grad

    @pl.when(step >= 6)
    def _():
        keep[0] = grad


def down_grad(info, act, dy):
    rows, width = dy.shape
    ff = act.shape[1]
    block = ff // 4
    chunk = block // 3

    def act_at(i, info):
        turn = i // 3
        owner = info[0] ^ ((turn & 1) * 2 + (1 - turn // 2))
        return (0, owner * 3 + i % 3)

    def send_at(i, info):
        i = jnp.minimum(i, 5)
        return (i // 3, i % 3, 0)

    def keep_at(i, info):
        i = jnp.maximum(i - 6, 0)
        return (i // 3, i % 3, 0)

    return pl.pallas_call(
        down_grad_kernel,
        grid_spec=pltpu.PrefetchScalarGridSpec(
            num_scalar_prefetch=1,
            grid=(12,),
            in_specs=[pl.BlockSpec((rows, chunk), act_at), whole((rows, width))],
            out_specs=[
                pl.BlockSpec((1, chunk, width), send_at),
                pl.BlockSpec((1, chunk, width), keep_at),
                whole((1, width)),
            ],
        ),
        out_shape=[
            jax.ShapeDtypeStruct((2, block, width), BF16),
            jax.ShapeDtypeStruct((2, block, width), BF16),
            jax.ShapeDtypeStruct((1, width), F32),
        ],
        compiler_params=pltpu.CompilerParams(
            vmem_limit_bytes=LIMIT, dimension_semantics=("arbitrary",)
        ),
        cost_estimate=pl.CostEstimate(
            flops=2 * rows * width * ff * 2, bytes_accessed=10000000, transcendentals=0
        ),
        name="down_grad",
    )(info, act, dy)


def transpose_by_owner(info, source, target):
    block = source.shape[1] // 4
    for owner in range(4):
        turned = source[:, owner * block : (owner + 1) * block].T
        near = owner ^ info[0]
        slot = (near & 1) * 2 + near // 2
        target[pl.ds(pl.multiple_of(slot * block, 16), block), :] = turned


def norm_grad_rows(values, incoming, gain):
    white, inverse = norm_parts(values)
    scaled = incoming * gain
    inner = (
        scaled
        - jnp.mean(scaled, axis=-1, keepdims=True)
        - white * jnp.mean(scaled * white, axis=-1, keepdims=True)
    )
    return (
        inner * inverse,
        jnp.sum(incoming * white, axis=0, keepdims=True),
        jnp.sum(incoming, axis=0, keepdims=True),
    )


def up_grad_kernel(info, slope, dy, second, hidden, vec, *refs):
    fc1_pieces, fc2_pieces = refs[:6], refs[6:12]
    keep, send, grad_hidden, branch, sums, bias_sums = refs[12:18]
    fc1_w, fc2_w, turned, grad_second, sems = refs[18:]
    step = pl.program_id(0)
    rows, width = dy.shape
    chunk = slope.shape[1]

    @pl.when(step == 0)
    def _():
        fc2_copies = weight_copies(info, fc2_pieces, fc2_w, sems.at[0])
        fc1_copies = weight_copies(info, fc1_pieces, fc1_w, sems.at[1])
        for copy in fc2_copies + fc1_copies:
            copy.start()
        transpose_by_owner(info, second, turned)
        for copy in fc2_copies + fc1_copies:
            copy.wait()

    columns = pl.ds(pl.multiple_of(step * chunk, chunk), chunk)
    grad_act = dot_nt(dy[...], fc2_w[columns, :])
    grad_pre = (grad_act * slope[...].astype(F32)).astype(BF16)
    bias_sums[...] = jnp.sum(grad_pre.astype(F32), axis=0, keepdims=True)
    grad = dot_nn(turned[...], grad_pre).astype(BF16).reshape(4, width // 4, chunk)
    keep[...] = grad[:2]
    send[...] = grad[2:]
    part = dot_nt(grad_pre, fc1_w[:, columns])

    @pl.when(step == 0)
    def _():
        grad_second[...] = part

    @pl.when(step > 0)
    def _():
        grad_second[...] += part

    @pl.when(step == pl.num_programs(0) - 1)
    def _():
        def norm_step(i, carry):
            at = pl.ds(pl.multiple_of(i * 128, 128), 128)
            through, gains, biases = norm_grad_rows(hidden[at, :], grad_second[at, :], vec[5:6, :])
            value = dy[at, :].astype(F32) + through
            grad_hidden[at, :] = value
            rounded = value.astype(BF16)
            branch[at, :] = rounded
            return (
                carry[0] + gains,
                carry[1] + biases,
                carry[2] + jnp.sum(rounded.astype(F32), axis=0, keepdims=True),
            )

        zero = jnp.zeros((1, width), F32)
        gains, biases, outs = lax.fori_loop(0, rows // 128, norm_step, (zero, zero, zero))
        sums[0:1, :] = gains
        sums[1:2, :] = biases
        sums[2:3, :] = outs


def up_grad(info, slope, dy, second, hidden, vec, fc1_pieces, fc2_pieces):
    rows, width = dy.shape
    ff = slope.shape[1]
    chunk = 512
    return pl.pallas_call(
        up_grad_kernel,
        grid=(ff // chunk,),
        in_specs=[
            pl.BlockSpec(memory_space=pltpu.SMEM),
            pl.BlockSpec((rows, chunk), lambda j: (0, j)),
            whole((rows, width)),
            whole((rows, width)),
            whole((rows, width)),
            whole(vec.shape),
        ]
        + [HBM] * 12,
        out_specs=[
            pl.BlockSpec((2, width // 4, chunk), lambda j: (0, 0, j)),
            pl.BlockSpec((2, width // 4, chunk), lambda j: (0, 0, j)),
            whole((rows, width)),
            whole((rows, width)),
            whole((3, width)),
            pl.BlockSpec((1, chunk), lambda j: (0, j)),
        ],
        out_shape=[
            jax.ShapeDtypeStruct((2, width // 4, ff), BF16),
            jax.ShapeDtypeStruct((2, width // 4, ff), BF16),
            jax.ShapeDtypeStruct((rows, width), F32),
            jax.ShapeDtypeStruct((rows, width), BF16),
            jax.ShapeDtypeStruct((3, width), F32),
            jax.ShapeDtypeStruct((1, ff), F32),
        ],
        scratch_shapes=[
            pltpu.VMEM((width, ff), BF16),
            pltpu.VMEM((ff, width), BF16),
            pltpu.VMEM((width, rows), BF16),
            pltpu.VMEM((rows, width), F32),
            pltpu.SemaphoreType.DMA((2, 6)),
        ],
        compiler_params=pltpu.CompilerParams(
            vmem_limit_bytes=LIMIT, dimension_semantics=("arbitrary",)
        ),
        cost_estimate=pl.CostEstimate(
            flops=2 * rows * width * ff * 6, bytes_accessed=30000000, transcendentals=0
        ),
        name="up_grad",
    )(info, slope, dy, second, hidden, vec, *fc1_pieces, *fc2_pieces)


def attend_grad_kernel(length, info, branch, mixed, first, packed, logsum, *refs):
    pieces = refs[:6]
    keep, send, grad_packed, sums = refs[6:10]
    weight, grad_mixed, turned, sems = refs[10:]
    rows, width = branch.shape
    copies = weight_copies(info, pieces, weight, sems)
    for copy in copies:
        copy.start()
    for copy in copies:
        copy.wait()

    def mixed_step(i, _):
        at = pl.ds(pl.multiple_of(i * 256, 256), 256)
        grad_mixed[at, :] = dot_nt(branch[at, :], weight[...]).astype(BF16)
        return 0

    lax.fori_loop(0, rows // 256, mixed_step, 0)

    pairs = width // 128
    blocks = length // 128
    causal = triangle(128)

    def pair_step(it, _):
        base = (it // pairs) * length
        column = (it % pairs) * 128
        at = pl.ds(pl.multiple_of(base, 128), length)
        at_query = pl.ds(pl.multiple_of(column, 128), 128)
        at_key = pl.ds(pl.multiple_of(width + column, 128), 128)
        at_value = pl.ds(pl.multiple_of(2 * width + column, 128), 128)
        query, key, value = packed[at, at_query], packed[at, at_key], packed[at, at_value]
        incoming = grad_mixed[at, at_query]
        lane = lax.broadcasted_iota(jnp.int32, query.shape, 1)
        results = []
        for head in range(2):
            here = (lane < HEAD) == (head == 0)
            query_h = jnp.where(here, query, jnp.zeros_like(query))
            incoming_h = jnp.where(here, incoming, jnp.zeros_like(incoming))
            probs, grads = [], []
            for kb in range(blocks):
                rows_k = slice(kb * 128, (kb + 1) * 128)
                scores = dot_nt(key[rows_k], query_h[kb * 128 :])
                stats = logsum[it * 2 + head, 0:1, kb * 128 :]
                expo = jnp.exp(scores - stats)
                diagonal = jnp.where(causal, expo[:, :128], 0.0)
                if kb < blocks - 1:
                    expo = jnp.concatenate([diagonal, expo[:, 128:]], axis=1)
                else:
                    expo = diagonal
                probs.append(expo)
                grads.append(dot_nt(value[rows_k], incoming_h[kb * 128 :]))
            inner = []
            for qb in range(blocks):
                total = None
                for kb in range(qb + 1):
                    cut = slice((qb - kb) * 128, (qb - kb + 1) * 128)
                    term = probs[kb][:, cut] * grads[kb][:, cut]
                    total = term if total is None else total + term
                inner.append(jnp.sum(total, axis=0, keepdims=True))
            inner = jnp.concatenate(inner, axis=1)
            score_grads = [
                (probs[kb] * (grads[kb] - inner[:, kb * 128 :])).astype(BF16)
                for kb in range(blocks)
            ]
            grad_values = [
                dot_nn(probs[kb].astype(BF16), incoming[kb * 128 :]) for kb in range(blocks)
            ]
            grad_keys = [dot_nn(score_grads[kb], query[kb * 128 :]) for kb in range(blocks)]
            grad_query = []
            for qb in range(blocks):
                tiles = [
                    score_grads[kb][:, (qb - kb) * 128 : (qb - kb + 1) * 128]
                    for kb in range(qb + 1)
                ]
                grad_query.append(dot_tn(key[: (qb + 1) * 128], jnp.concatenate(tiles, axis=0)))
            results.append((grad_values, grad_keys, grad_query))
        left = lax.broadcasted_iota(jnp.int32, (128, 128), 1) < HEAD
        for b in range(blocks):
            to = pl.ds(pl.multiple_of(base + b * 128, 128), 128)
            grad_packed[to, at_value] = jnp.where(left, results[0][0][b], results[1][0][b]).astype(
                BF16
            )
            grad_packed[to, at_key] = jnp.where(left, results[0][1][b], results[1][1][b]).astype(
                BF16
            )
            both = jnp.concatenate([results[0][2][b][:HEAD], results[1][2][b][HEAD:]], axis=0)
            grad_packed[to, at_query] = (both.T * HEAD**-0.5).astype(BF16)
        return 0

    lax.fori_loop(0, (rows // length) * pairs, pair_step, 0)

    def weight_grad(source, source_at, target_at):
        grad = dot_nn(turned[...], source[:, source_at]).astype(BF16).reshape(4, width // 4, 256)
        keep[:, :, target_at] = grad[:2]
        send[:, :, target_at] = grad[2:]

    transpose_by_owner(info, mixed, turned)

    def out_step(i, _):
        weight_grad(
            branch,
            pl.ds(pl.multiple_of(i * 256, 256), 256),
            pl.ds(pl.multiple_of(3 * width + i * 256, 256), 256),
        )
        return 0

    lax.fori_loop(0, width // 256, out_step, 0)
    transpose_by_owner(info, first, turned)

    def packed_step(i, _):
        at = pl.ds(pl.multiple_of(i * 256, 256), 256)
        weight_grad(grad_packed, at, at)
        sums[:, at] = jnp.sum(grad_packed[:, at].astype(F32), axis=0, keepdims=True)
        return 0

    lax.fori_loop(0, 3 * width // 256, packed_step, 0)


def attend_grad(info, branch, mixed, first, packed, logsum, pieces, length):
    rows, width = branch.shape
    return pl.pallas_call(
        partial(attend_grad_kernel, length),
        in_specs=[pl.BlockSpec(memory_space=pltpu.SMEM)]
        + [pl.BlockSpec(memory_space=pltpu.VMEM)] * 5
        + [HBM] * 6,
        out_specs=[pl.BlockSpec(memory_space=pltpu.VMEM)] * 4,
        out_shape=[
            jax.ShapeDtypeStruct((2, width // 4, 4 * width), BF16),
            jax.ShapeDtypeStruct((2, width // 4, 4 * width), BF16),
            jax.ShapeDtypeStruct((rows, 3 * width), BF16),
            jax.ShapeDtypeStruct((1, 3 * width), F32),
        ],
        scratch_shapes=[
            pltpu.VMEM((width, width), BF16),
            pltpu.VMEM((rows, width), BF16),
            pltpu.VMEM((width, rows), BF16),
            pltpu.SemaphoreType.DMA((6,)),
        ],
        compiler_params=pltpu.CompilerParams(vmem_limit_bytes=LIMIT),
        cost_estimate=pl.CostEstimate(
            flops=2 * rows * width * 4 * width * 6, bytes_accessed=20000000, transcendentals=0
        ),
        name="attend_grad",
    )(info, branch, mixed, first, packed, logsum, *pieces)


def input_grad_kernel(info, grad_packed, tok, grad_hidden, vec, *refs):
    pieces, (in_grad, sums), (weight, sems) = refs[:6], refs[6:8], refs[8:]
    rows, width = tok.shape
    step = pl.program_id(0)

    @pl.when(step == 0)
    def _():
        copies = weight_copies(info, pieces, weight, sems)
        for copy in copies:
            copy.start()
        sums[...] = jnp.zeros_like(sums)
        for copy in copies:
            copy.wait()

    grad_first = dot_nt(grad_packed[...], weight[...])
    through, gains, biases = norm_grad_rows(tok[...].astype(F32), grad_first, vec[0:1, :])
    in_grad[...] = (grad_hidden[...] + through).astype(BF16)
    sums[0:1, :] += gains
    sums[1:2, :] += biases


def input_grad(info, grad_packed, tok, grad_hidden, vec, pieces):
    rows, width = tok.shape
    block = 256
    return pl.pallas_call(
        input_grad_kernel,
        grid=(rows // block,),
        in_specs=[
            pl.BlockSpec(memory_space=pltpu.SMEM),
            pl.BlockSpec((block, 3 * width), lambda i: (i, 0)),
            pl.BlockSpec((block, width), lambda i: (i, 0)),
            pl.BlockSpec((block, width), lambda i: (i, 0)),
            whole(vec.shape),
        ]
        + [HBM] * 6,
        out_specs=[pl.BlockSpec((block, width), lambda i: (i, 0)), whole((2, width))],
        out_shape=[
            jax.ShapeDtypeStruct((rows, width), BF16),
            jax.ShapeDtypeStruct((2, width), F32),
        ],
        scratch_shapes=[pltpu.VMEM((width, 3 * width), BF16), pltpu.SemaphoreType.DMA((6,))],
        compiler_params=pltpu.CompilerParams(
            vmem_limit_bytes=LIMIT, dimension_semantics=("arbitrary",)
        ),
        cost_estimate=pl.CostEstimate(
            flops=2 * rows * width * 3 * width * 2, bytes_accessed=14000000, transcendentals=0
        ),
        name="input_grad",
    )(info, grad_packed, tok, grad_hidden, vec, *pieces)


def output_kernel(info, act, hidden, vec, *refs):
    pieces, (out,), (weight, sems) = refs[:6], refs[6:7], refs[7:]

    @pl.when(pl.program_id(0) == 0)
    def _():
        copies = weight_copies(info, pieces, weight, sems)
        for copy in copies:
            copy.start()
        for copy in copies:
            copy.wait()

    out[...] = (hidden[...] + dot_nn(act[...], weight[...]) + vec[7:8, :]).astype(BF16)


def output_rows(info, act, hidden, vec, pieces):
    rows, width = hidden.shape
    ff = act.shape[1]
    block = 256
    return pl.pallas_call(
        output_kernel,
        grid=(rows // block,),
        in_specs=[
            pl.BlockSpec(memory_space=pltpu.SMEM),
            pl.BlockSpec((block, ff), lambda i: (i, 0)),
            pl.BlockSpec((block, width), lambda i: (i, 0)),
            whole(vec.shape),
        ]
        + [HBM] * 6,
        out_specs=pl.BlockSpec((block, width), lambda i: (i, 0)),
        out_shape=jax.ShapeDtypeStruct((rows, width), BF16),
        scratch_shapes=[pltpu.VMEM((ff, width), BF16), pltpu.SemaphoreType.DMA((6,))],
        compiler_params=pltpu.CompilerParams(
            vmem_limit_bytes=LIMIT, dimension_semantics=("arbitrary",)
        ),
        cost_estimate=pl.CostEstimate(
            flops=2 * rows * width * ff * 2, bytes_accessed=14000000, transcendentals=0
        ),
        name="output_rows",
    )(info, act, hidden, vec, *pieces)


def swap(value, axis, size, bit):
    return lax.ppermute(value, axis, [(i, i ^ bit) for i in range(size)])


def gather_weight(block, reps, half):
    part = block.shape[0] // 2
    mine = lax.dynamic_slice_in_dim(block, half * part, part, 0)
    far_a = swap(mine, "shard", 4, 2)
    far_b = swap(far_a, "rep", reps, 1)
    return (
        block,
        swap(block, "shard", 4, 1),
        far_a,
        far_b,
        swap(far_a, "shard", 4, 1),
        swap(far_b, "shard", 4, 1),
    )


def halves(terms, bit, axis=0):
    size = terms[0].shape[axis] // 2

    def cut(start):
        total = None
        for term in terms:
            piece = lax.dynamic_slice_in_dim(term, start, size, axis).astype(F32)
            total = piece if total is None else total + piece
        return total.astype(BF16)

    return cut(bit * size), cut((1 - bit) * size)


def reduce_chunk(keep, send, me, rep, reps):
    got = swap(send, "shard", 4, 1)
    far = (keep[1].astype(F32) + got[1].astype(F32)).astype(BF16)
    far = swap(far, "shard", 4, 2)
    terms = [keep[0], got[0], far]
    bits = reps.bit_length() - 1
    for level in range(bits):
        mine, other = halves(terms, (rep >> level) & 1)
        terms = [mine, swap(other, "rep", reps, 1 << level)]
    total = sum(term.astype(F32) for term in terms).astype(BF16)
    for level in reversed(range(bits)):
        other = swap(total, "rep", reps, 1 << level)
        bit = (rep >> level) & 1
        total = jnp.where(
            bit == 0,
            jnp.concatenate([total, other], axis=0),
            jnp.concatenate([other, total], axis=0),
        )
    return total.astype(F32)


def sum_small(value, reps):
    value = value + swap(value, "shard", 4, 1)
    value = value + swap(value, "shard", 4, 2)
    bit = 1
    while bit < reps:
        value = value + swap(value, "rep", reps, bit)
        bit *= 2
    return value


def on_device(
    reps,
    tokens,
    ln1_gain,
    ln1_bias,
    qkv_weight,
    query_bias,
    value_bias,
    out_weight,
    out_bias,
    ln2_gain,
    ln2_bias,
    fc1_weight,
    fc1_bias,
    fc2_weight,
    fc2_bias,
    cotangent,
):
    seqs_here, length, width = tokens.shape
    rows = seqs_here * length
    me = lax.axis_index("shard").astype(jnp.int32)
    rep = lax.axis_index("rep").astype(jnp.int32)
    half = rep & 1
    info = jnp.stack([me, half])

    small = jnp.concatenate(
        [
            ln1_gain,
            ln1_bias,
            query_bias,
            value_bias,
            out_bias,
            ln2_gain,
            ln2_bias,
            fc2_bias,
            fc1_bias,
        ]
    ).reshape(1, -1)
    pair = jnp.concatenate([small, swap(small, "shard", 4, 1)], axis=0)
    near = jnp.concatenate([pair, swap(pair, "shard", 4, 2)], axis=0)
    near = jnp.where((me & 1) == 0, near, near[jnp.array([1, 0, 3, 2])])
    near = jnp.where((me & 2) == 0, near, near[jnp.array([2, 3, 0, 1])]).astype(F32)
    share = width // 4
    vec = near[:, : 8 * share].reshape(4, 8, share).transpose(1, 0, 2).reshape(8, width)
    bias = near[:, 8 * share :].reshape(1, -1)

    qkv = gather_weight(qkv_weight, reps, half)
    out = gather_weight(out_weight, reps, half)
    fc1 = gather_weight(fc1_weight, reps, half)
    fc2 = gather_weight(fc2_weight, reps, half)

    tok = tokens.reshape(rows, width)
    dy = cotangent.reshape(rows, width)
    first, packed, mixed, logsum = attend(info, tok, vec, qkv, length)
    hidden, second, act, slope = feed(info, mixed, tok, vec, bias, out, fc1)
    send2, keep2, sums_dy = down_grad(info, act, dy)
    keep1, send1, grad_hidden, branch, sums_ln2, sums_fc1 = up_grad(
        info, slope, dy, second, hidden, vec, fc1, fc2
    )
    keep0, send0, grad_packed, sums_packed = attend_grad(
        info, branch, mixed, first, packed, logsum, out, length
    )
    in_grad, sums_ln1 = input_grad(info, grad_packed, tok, grad_hidden, vec, qkv)
    output = output_rows(info, act, hidden, vec, fc2)

    total2 = reduce_chunk(keep2, send2, me, rep, reps)
    total1 = reduce_chunk(keep1, send1, me, rep, reps)
    total0 = reduce_chunk(keep0, send0, me, rep, reps)

    sums = jnp.concatenate(
        [
            sums_ln1,
            sums_packed.reshape(3, width),
            sums_ln2,
            sums_dy,
            sums_fc1.reshape(4, width),
        ],
        axis=0,
    )
    sums = sum_small(sums, reps)
    mine = lax.dynamic_slice_in_dim(sums, me * share, share, 1)
    fc1b = lax.dynamic_slice_in_dim(sums, 9 + me, 1, 0).reshape(width)
    return (
        output.reshape(tokens.shape),
        in_grad.reshape(tokens.shape),
        mine[0],
        mine[1],
        total0[:, : 3 * width],
        mine[2],
        mine[4],
        total0[:, 3 * width :],
        mine[7],
        mine[5],
        mine[6],
        total1,
        fc1b,
        total2,
        mine[8],
    )


def solution(mesh):
    spread = P(("rep", "shard"), None, None)
    matrix = P("shard", None)
    vector = P("shard")
    return jax.shard_map(
        partial(on_device, mesh.shape["rep"]),
        mesh=mesh,
        in_specs=(
            spread, vector, vector, matrix, vector, vector, matrix, vector,
            vector, vector, matrix, vector, matrix, vector, spread,
        ),
        out_specs=(
            spread, spread, vector, vector, matrix, vector, vector, matrix,
            vector, vector, vector, matrix, vector, matrix, vector,
        ),
        check_vma=False,
    )
```

time: 665 us -> 405 us (0.61); the launches traced: 656 us -> 404 us
  blocking collectives: 309 us -> 0 us
  matrix products: 145 us -> 0 us
  Pallas kernels: 0 us -> 125 us
  waiting for transfers between devices: 94.9 us -> 186 us
  starting transfers between devices: 0.32 us -> 42.3 us
  other arithmetic: 49 us -> 20.5 us
  between operations: 17 us -> 1.16 us
  local copies, waits for them, and re-layouts: 40.9 us -> 28.1 us
    psum x1 -> x0, blocking collectives: 279 us -> none  [on_device(): lax.psum((owned_g1, owned_b1, owned_qkv, owned_qb, owned_vb, owned_ow, ow...]
    ppermute x0 -> x51, waiting for transfers between devices: none -> 186 us  [swap(): return lax.ppermute(value, axis, [(i, i ^ bit) for i in range(size)])]
    dot_general x18 -> x0, matrix products: 145 us -> none  [the longest x4 41.9 us: matmul_plain(): return jnp.dot(left, right, preferred_element_type=jnp.float32)]
    pallas_call x0 -> x7, Pallas kernels: none -> 125 us  [the longest x1 28.8 us: attend_grad(): pl.pallas_call(partial(attend_grad_kernel, length), in_specs=[pl.BlockSpe...]
    reduce_scatter x4 -> x0, waiting for transfers between devices: 66.1 us -> none  [the longest x1 50.6 us: on_device(): lax.psum_scatter(grad_fc2w.astype(jnp.bfloat16), 'shard', scatter_dimensi...]
    ppermute x0 -> x51, starting transfers between devices: none -> 42.3 us  [swap(): return lax.ppermute(value, axis, [(i, i ^ bit) for i in range(size)])]
    all_gather x4 -> x0, waiting for transfers between devices: 26.2 us -> none  [the longest x1 16.9 us: on_device(): lax.all_gather(fc2_weight, 'shard', axis=0, tiled=True)]
    unnamed x2 -> x0, blocking collectives: 25 us -> none
  transfers between devices with their start and end apart: 8 -> 51, of which waited for: 5 -> 25; matrix products, arithmetic and copies ran while one was open for 30% -> 9% of each run, Pallas kernels for 0% -> 18%
where the time goes in v1:
time: 405 us; the launch traced here: 404 us
  waiting for transfers between devices  186 us (46%)
  Pallas kernels  125 us (31%)
  starting transfers between devices  42.3 us (10%)
  local copies, waits for them, and re-layouts  28.1 us (7%)
  other arithmetic  20.5 us (5%)
    ppermute x51, waiting for transfers between devices, swap(): return lax.ppermute(value, axis, [(i, i ^ bit) for i in range(size)])  186 us
    ppermute x51, starting transfers between devices, swap(): return lax.ppermute(value, axis, [(i, i ^ bit) for i in range(size)])  42.3 us
    pallas_call x1, Pallas kernels, attend_grad(): pl.pallas_call(partial(attend_grad_kernel, length), in_specs=[pl.BlockSpe...  28.8 us
    pallas_call x1, Pallas kernels, up_grad(): pl.pallas_call(up_grad_kernel, grid=(ff // chunk,), in_specs=[pl.BlockSpe...  25.3 us
    pallas_call x1, Pallas kernels, attend(): pl.pallas_call(partial(attend_kernel, length), in_specs=[pl.BlockSpec(mem...  20.6 us
    pallas_call x1, Pallas kernels, feed(): pl.pallas_call(feed_kernel, grid=(ff // chunk,), in_specs=[pl.BlockSpec(m...  18.6 us
    pallas_call x1, Pallas kernels, down_grad(): pl.pallas_call(down_grad_kernel, grid_spec=pltpu.PrefetchScalarGridSpec(n...  13.3 us
    pallas_call x1, Pallas kernels, output_rows(): pl.pallas_call(output_kernel, grid=(rows // block,), in_specs=[pl.BlockSp...  9.48 us
  transfers between devices with their start and end apart: 51, of which 25 were waited for; matrix products, arithmetic and copies ran while one was open for 9% of the time, Pallas kernels for 18%

profile of v1, /device:TPU:0, one launch (start us, length us, event | category | flops | bytes accessed | tf_op | source)
XLA Modules:
  0.0 403.5 jit_solution(7229134028007174334)
XLA Ops:
  0.6 6.1 %concatenate.67 = bf16[2304]{0:T(1024)(128)(2,1)S(1)} concatenate(bf16[192]{0:T(256)(128)(2,1)} %param.18, bf16[192]{0:T(256)(128)(2,1)} %param.19, bf16[192]{0:T(256)(128)(2,1)} %param.21, bf16[192]{0:T(256)(128)(2,1)} %param.22, bf16[192]{0:T(256)(128)(2,1)} %param.24, bf16[192]{0:T(256)(128)(2,1)} %param.25, bf16[192]{0:T(256)(128)(2,1)} %param.26, bf16[192]{0:T(256)(128)(2,1)} %param.30, ...), dimensions={0} | concatenate | bytes 9216 | tf_op jit(solution)/shard_map/concatenate | solution.py:786
  16.5 21.3 %collective-permute-done.1 = bf16[2,2304]{1,0:T(2,128)(2,1)S(1)} collective-permute-done((bf16[2,2304]{1,0:T(2,128)(2,1)S(1)}, bf16[2,2304]{1,0:T(2,128)(2,1)S(1)}, u32[]{:S(2)}, u32[]{:S(2)}) %collective-permute-start.1) | collective-permute-done | bytes 9248 | tf_op jit(solution)/shard_map/ppermute | solution.py:699
  46.5 8.2 %collective-permute-done.13.refs_8_.refs_2_ = bf16[96,3072]{1,0:T(8,128)(2,1)} collective-permute-done((bf16[96,3072]{1,0:T(8,128)(2,1)S(1)}, bf16[96,3072]{1,0:T(8,128)(2,1)}, u32[]{:S(2)}, u32[]{:S(2)}) %collective-permute-start.13) | collective-permute-done | bytes 589856 | tf_op jit(solution)/shard_map/ppermute | solution.py:699
  58.3 10.3 %collective-permute-done.14.refs_9_.refs_3_ = bf16[96,3072]{1,0:T(8,128)(2,1)S(1)} collective-permute-done((bf16[96,3072]{1,0:T(8,128)(2,1)}, bf16[96,3072]{1,0:T(8,128)(2,1)S(1)}, u32[]{:S(2)}, u32[]{:S(2)}) %collective-permute-start.14) | collective-permute-done | bytes 589856 | tf_op jit(solution)/shard_map/ppermute | solution.py:699
  70.3 20.6 %attend.1 = (bf16[768,768]{1,0:T(8,128)(2,1)}, bf16[768,2304]{1,0:T(8,128)(2,1)}, bf16[768,768]{1,0:T(8,128)(2,1)}, f32[24,1,384]{2,1,0:T(1,128)}) custom-call(s32[2]{0:T(128)} %pad_add_fusion.info, bf16[768,768]{1,0:T(8,128)(2,1)} %bitcast.63, f32[8,768]{1,0:T(8,128)} %reshape.108.vec, bf16[192,2304]{1,0:T(8,128)(2,1)} %refs_0_.11, ...), custom_call_target="tpu_custom_call" | custom-call | flops 8153726976 | bytes 12000000 | tf_op jit(solution)/shard_map/attend/pallas_call | solution.py:159
  92.6 18.6 %feed.1 = (f32[768,768]{1,0:T(8,128)}, bf16[768,768]{1,0:T(8,128)(2,1)}, bf16[768,3072]{1,0:T(8,128)(2,1)}, bf16[768,3072]{1,0:T(8,128)(2,1)}) custom-call(s32[2]{0:T(128)} %pad_add_fusion.info, bf16[768,768]{1,0:T(8,128)(2,1)} %get-tuple-element.38.mixed, bf16[768,768]{1,0:T(8,128)(2,1)} %bitcast.64, f32[8,768]{1,0:T(8,128)} %reshape.108.vec, ...), custom_call_target="tpu_custom_call" | custom-call | flops 9059696640 | bytes 20000000 | tf_op jit(solution)/shard_map/feed/pallas_call | solution.py:229
  112.6 25.3 %up_grad.1 = (bf16[2,192,3072]{2,1,0:T(8,128)(2,1)}, bf16[2,192,3072]{2,1,0:T(8,128)(2,1)}, f32[768,768]{1,0:T(8,128)}, bf16[768,768]{1,0:T(8,128)(2,1)}, f32[3,768]{1,0:T(4,128)}, /*index=5*/f32[1,3072]{1,0:T(1,128)}) custom-call(s32[2]{0:T(128)} %pad_add_fusion.info, bf16[768,3072]{1,0:T(8,128)(2,1)} %get-tuple-element.41.slope, ...), custom_call_target="tpu_custom_call" | custom-call | flops 21743271936 | bytes 30000000 | tf_op jit(solution)/shard_map/up_grad/pallas_call | solution.py:416
  137.9 28.8 %attend_grad.1 = (bf16[2,192,3072]{2,1,0:T(8,128)(2,1)}, bf16[2,192,3072]{2,1,0:T(8,128)(2,1)}, bf16[768,2304]{1,0:T(8,128)(2,1)}, f32[1,2304]{1,0:T(1,128)}) custom-call(s32[2]{0:T(128)} %pad_add_fusion.info, bf16[768,768]{1,0:T(8,128)(2,1)} %get-tuple-element.43.branch, bf16[768,768]{1,0:T(8,128)(2,1)} %get-tuple-element.38.mixed, ...), custom_call_target="tpu_custom_call" | custom-call | flops 21743271936 | bytes 20000000 | tf_op jit(solution)/shard_map/attend_grad/pallas_call | solution.py:580
  167.1 13.3 %down_grad.1 = (bf16[2,768,768]{2,1,0:T(8,128)(2,1)}, bf16[2,768,768]{2,1,0:T(8,128)(2,1)}, f32[1,768]{1,0:T(1,128)}) custom-call(s32[2]{0:T(128)} %pad_add_fusion.info, bf16[768,3072]{1,0:T(8,128)(2,1)} %get-tuple-element.39.act, bf16[768,768]{1,0:T(8,128)(2,1)} %bitcast.62), custom_call_target="tpu_custom_call" | custom-call | flops 7247757312 | bytes 10000000 | tf_op jit(solution)/shard_map/down_grad/pallas_call | solution.py:304
  196.9 9.3 %input_grad.1 = (bf16[768,768]{1,0:T(8,128)(2,1)}, f32[2,768]{1,0:T(2,128)}) custom-call(s32[2]{0:T(128)} %pad_add_fusion.info, bf16[768,2304]{1,0:T(8,128)(2,1)} %get-tuple-element.47.grad_packed, bf16[768,768]{1,0:T(8,128)(2,1)} %bitcast.65, f32[768,768]{1,0:T(8,128)} %get-tuple-element.48.grad_hidden, f32[8,768]{1,0:T(8,128)} %reshape.108.vec, ...), custom_call_target="tpu_custom_call" | custom-call | flops 5435817984 | bytes 14000000 | tf_op jit(solution)/shard_map/input_grad/pallas_call | solution.py:630
  211.1 51.5 %collective-permute-done.23 = f32[13,768]{1,0:T(8,128)S(1)} collective-permute-done((f32[13,768]{1,0:T(8,128)S(1)}, f32[13,768]{1,0:T(8,128)S(1)}, u32[]{:S(2)}, u32[]{:S(2)}) %collective-permute-start.23) | collective-permute-done | bytes 39968 | tf_op jit(solution)/shard_map/ppermute | solution.py:699
  263.1 3.7 collective-permute-done.24
  285.0 9.5 %output_rows.1 = bf16[768,768]{1,0:T(8,128)(2,1)} custom-call(s32[2]{0:T(128)} %pad_add_fusion.info, bf16[768,3072]{1,0:T(8,128)(2,1)} %get-tuple-element.39.act, f32[768,768]{1,0:T(8,128)} %get-tuple-element.40.hidden, f32[8,768]{1,0:T(8,128)} %reshape.108.vec, bf16[768,768]{1,0:T(8,128)(2,1)} %refs_6_.3, bf16[768,768]{1,0:T(8,128)(2,1)} %copy-done.13, ...), custom_call_target="tpu_custom_call" | custom-call | flops 7247757312 | bytes 14000000 | tf_op jit(solution)/shard_map/output_rows/pallas_call | solution.py:675
  297.1 11.8 %collective-permute-done.45 = bf16[384,768]{1,0:T(8,128)(2,1)S(1)} collective-permute-done((bf16[384,768]{1,0:T(8,128)(2,1)S(1)}, bf16[384,768]{1,0:T(8,128)(2,1)S(1)}, u32[]{:S(2)}, u32[]{:S(2)}) %collective-permute-start.45) | collective-permute-done | bytes 589856 | tf_op jit(solution)/shard_map/ppermute | solution.py:699
  309.7 8.4 %collective-permute-done.37 = bf16[96,3072]{1,0:T(8,128)(2,1)S(1)} collective-permute-done((bf16[96,3072]{1,0:T(8,128)(2,1)S(1)}, bf16[96,3072]{1,0:T(8,128)(2,1)S(1)}, u32[]{:S(2)}, u32[]{:S(2)}) %collective-permute-start.37) | collective-permute-done | bytes 589856 | tf_op jit(solution)/shard_map/ppermute | solution.py:699
  321.9 7.1 %collective-permute-done.38 = bf16[48,3072]{1,0:T(8,128)(2,1)S(1)} collective-permute-done((bf16[48,3072]{1,0:T(8,128)(2,1)S(1)}, bf16[48,3072]{1,0:T(8,128)(2,1)S(1)}, u32[]{:S(2)}, u32[]{:S(2)}) %collective-permute-start.38) | collective-permute-done | bytes 294944 | tf_op jit(solution)/shard_map/ppermute | solution.py:699
  332.2 6.7 %collective-permute-done.47 = bf16[96,768]{1,0:T(8,128)(2,1)S(1)} collective-permute-done((bf16[96,768]{1,0:T(8,128)(2,1)S(1)}, bf16[96,768]{1,0:T(8,128)(2,1)S(1)}, u32[]{:S(2)}, u32[]{:S(2)}) %collective-permute-start.47) | collective-permute-done | bytes 147488 | tf_op jit(solution)/shard_map/ppermute | solution.py:699
  339.1 3.0 collective-permute-done.39
  342.2 7.8 %collective-permute-done.32 = bf16[24,3072]{1,0:T(8,128)(2,1)S(1)} collective-permute-done((bf16[24,3072]{1,0:T(8,128)(2,1)S(1)}, bf16[24,3072]{1,0:T(8,128)(2,1)S(1)}, u32[]{:S(2)}, u32[]{:S(2)}) %collective-permute-start.32) | collective-permute-done | bytes 147488 | tf_op jit(solution)/shard_map/ppermute | solution.py:699
  357.3 4.6 %collective-permute-done.33 = bf16[48,3072]{1,0:T(8,128)(2,1)S(1)} collective-permute-done((bf16[48,3072]{1,0:T(8,128)(2,1)S(1)}, bf16[48,3072]{1,0:T(8,128)(2,1)S(1)}, u32[]{:S(2)}, u32[]{:S(2)}) %collective-permute-start.33) | collective-permute-done | bytes 294944 | tf_op jit(solution)/shard_map/ppermute | solution.py:699
  362.6 5.6 %collective-permute-done.49 = bf16[192,768]{1,0:T(8,128)(2,1)S(1)} collective-permute-done((bf16[192,768]{1,0:T(8,128)(2,1)S(1)}, bf16[192,768]{1,0:T(8,128)(2,1)S(1)}, u32[]{:S(2)}, u32[]{:S(2)}) %collective-permute-start.49) | collective-permute-done | bytes 294944 | tf_op jit(solution)/shard_map/ppermute | solution.py:699
  368.9 5.1 %collective-permute-done.41 = bf16[48,3072]{1,0:T(8,128)(2,1)S(1)} collective-permute-done((bf16[48,3072]{1,0:T(8,128)(2,1)S(1)}, bf16[48,3072]{1,0:T(8,128)(2,1)S(1)}, u32[]{:S(2)}, u32[]{:S(2)}) %collective-permute-start.41) | collective-permute-done | bytes 294944 | tf_op jit(solution)/shard_map/ppermute | solution.py:699
  380.8 10.2 %collective-permute-done.50 = bf16[384,768]{1,0:T(8,128)(2,1)S(1)} collective-permute-done((bf16[384,768]{1,0:T(8,128)(2,1)S(1)}, bf16[384,768]{1,0:T(8,128)(2,1)S(1)}, u32[]{:S(2)}, u32[]{:S(2)}) %collective-permute-start.50) | collective-permute-done | bytes 589856 | tf_op jit(solution)/shard_map/ppermute | solution.py:699
  392.6 9.3 %collective-permute-done.42 = bf16[96,3072]{1,0:T(8,128)(2,1)S(1)} collective-permute-done((bf16[96,3072]{1,0:T(8,128)(2,1)S(1)}, bf16[96,3072]{1,0:T(8,128)(2,1)S(1)}, u32[]{:S(2)}, u32[]{:S(2)}) %collective-permute-start.42) | collective-permute-done | bytes 589856 | tf_op jit(solution)/shard_map/ppermute | solution.py:699
  (196 shorter events, 96.2 us)
Async XLA Ops:
  7.3 38.5 %collective-permute-start.7 = (bf16[192,768]{1,0:T(8,128)(2,1)}, bf16[192,768]{1,0:T(8,128)(2,1)}, u32[]{:S(2)}, u32[]{:S(2)}) collective-permute-start(bf16[192,768]{1,0:T(8,128)(2,1)} %refs_0_.10), channel_id=1, source_target_pairs={{0,1},{1,0},{2,3},{3,2},{4,5},{5,4},{6,7},{7,6},{8,9},{9,8},{10,11... | collective-permute-start | bytes 884744 | tf_op jit(solution)/shard_map/ppermute | solution.py:699
  12.4 31.0 %collective-permute-start.3 = (bf16[96,2304]{1,0:T(8,128)(2,1)S(1)}, bf16[96,2304]{1,0:T(8,128)(2,1)S(1)}, u32[]{:S(2)}, u32[]{:S(2)}) collective-permute-start(bf16[96,2304]{1,0:T(8,128)(2,1)S(1)} %constant_dynamic-slice_fusion.5), channel_id=1, source_target_pairs={{0,2},{1,3},{2,0},{3,1},{4,6},{5,7},{6,4},{7,5},{8,10},{9,11},{10,... | collective-permute-start | bytes 1327112 | tf_op jit(solution)/shard_map/ppermute | solution.py:699
  13.6 32.7 %collective-permute-start.18 = (bf16[384,768]{1,0:T(8,128)(2,1)S(1)}, bf16[384,768]{1,0:T(8,128)(2,1)}, u32[]{:S(2)}, u32[]{:S(2)}) collective-permute-start(bf16[384,768]{1,0:T(8,128)(2,1)S(1)} %constant_dynamic-slice_fusion.2), channel_id=1, source_target_pairs={{0,2},{1,3},{2,0},{3,1},{4,6},{5,7},{6,4},{7,5},{8,10},{9,11},{10,... | collective-permute-start | bytes 1769480 | tf_op jit(solution)/shard_map/ppermute | solution.py:699
  15.8 21.9 %collective-permute-start.1 = (bf16[2,2304]{1,0:T(2,128)(2,1)S(1)}, bf16[2,2304]{1,0:T(2,128)(2,1)S(1)}, u32[]{:S(2)}, u32[]{:S(2)}) collective-permute-start(bf16[2,2304]{1,0:T(2,128)(2,1)S(1)} %pad_maximum_fusion.1), channel_id=1, source_target_pairs={{0,2},{1,3},{2,0},{3,1},{4,6},{5,7},{6,4},{7,5},{8,10},{9,11},{10,... | collective-permute-start | bytes 27656 | tf_op jit(solution)/shard_map/ppermute | solution.py:699
  16.5 23.6 %collective-permute-start.10 = (bf16[96,768]{1,0:T(8,128)(2,1)}, bf16[96,768]{1,0:T(8,128)(2,1)}, u32[]{:S(2)}, u32[]{:S(2)}) collective-permute-start(bf16[96,768]{1,0:T(8,128)(2,1)} %collective-permute-done.8.refs_2_), channel_id=1, source_target_pairs={{0,1},{1,0},{2,3},{3,2},{4,5},{5,4},{6,7},{7,6},{8,9},{9,8},{10,11... | collective-permute-start | bytes 442376 | tf_op jit(solution)/shard_map/ppermute | solution.py:699
  46.0 45.6 %collective-permute-start.12 = (bf16[192,3072]{1,0:T(8,128)(2,1)S(1)}, bf16[192,3072]{1,0:T(8,128)(2,1)}, u32[]{:S(2)}, u32[]{:S(2)}) collective-permute-start(bf16[192,3072]{1,0:T(8,128)(2,1)S(1)} %copy-done.8), channel_id=1, source_target_pairs={{0,1},{1,0},{2,3},{3,2},{4,5},{5,4},{6,7},{7,6},{8,9},{9,8},{10,11... | collective-permute-start | bytes 3538952 | tf_op jit(solution)/shard_map/ppermute | solution.py:699
  57.7 53.5 %collective-permute-start.17 = (bf16[768,768]{1,0:T(8,128)(2,1)}, bf16[768,768]{1,0:T(8,128)(2,1)S(1)}, u32[]{:S(2)}, u32[]{:S(2)}) collective-permute-start(bf16[768,768]{1,0:T(8,128)(2,1)} %refs_6_.3), channel_id=1, source_target_pairs={{0,1},{1,0},{2,3},{3,2},{4,5},{5,4},{6,7},{7,6},{8,9},{9,8},{10,11... | collective-permute-start | bytes 3538952 | tf_op jit(solution)/shard_map/ppermute | solution.py:699
  58.2 33.3 %collective-permute-start.15 = (bf16[96,3072]{1,0:T(8,128)(2,1)}, bf16[96,3072]{1,0:T(8,128)(2,1)S(1)}, u32[]{:S(2)}, u32[]{:S(2)}) collective-permute-start(bf16[96,3072]{1,0:T(8,128)(2,1)} %collective-permute-done.13.refs_8_.refs_2_), channel_id=1, source_target_pairs={{0,1},{1,0},{2,3},{3,2},{4,5},{5,4},{6,7},{7,6},{8,9},{9,8},{10,11... | collective-permute-start | bytes 1769480 | tf_op jit(solution)/shard_map/ppermute | solution.py:699
  68.6 22.3 %collective-permute-start.19 = (bf16[384,768]{1,0:T(8,128)(2,1)}, bf16[384,768]{1,0:T(8,128)(2,1)S(1)}, u32[]{:S(2)}, u32[]{:S(2)}) collective-permute-start(bf16[384,768]{1,0:T(8,128)(2,1)} %collective-permute-done.18.refs_2_.refs_8_), channel_id=1, source_target_pairs={{0,4},{4,0},{8,12},{12,8},{16,20},{20,16},{24,28},{28,24},{1,5},{5... | collective-permute-start | bytes 1769480 | tf_op jit(solution)/shard_map/ppermute | solution.py:699
  70.3 21.3 %collective-permute-start.16 = (bf16[96,3072]{1,0:T(8,128)(2,1)S(1)}, bf16[96,3072]{1,0:T(8,128)(2,1)S(1)}, u32[]{:S(2)}, u32[]{:S(2)}) collective-permute-start(bf16[96,3072]{1,0:T(8,128)(2,1)S(1)} %collective-permute-done.14.refs_9_.refs_3_), channel_id=1, source_target_pairs={{0,1},{1,0},{2,3},{3,2},{4,5},{5,4},{6,7},{7,6},{8,9},{9,8},{10,11... | collective-permute-start | bytes 1769480 | tf_op jit(solution)/shard_map/ppermute | solution.py:699
  91.0 20.3 %collective-permute-start.20 = (bf16[384,768]{1,0:T(8,128)(2,1)}, bf16[384,768]{1,0:T(8,128)(2,1)S(1)}, u32[]{:S(2)}, u32[]{:S(2)}) collective-permute-start(bf16[384,768]{1,0:T(8,128)(2,1)} %collective-permute-done.18.refs_2_.refs_8_), channel_id=1, source_target_pairs={{0,1},{1,0},{2,3},{3,2},{4,5},{5,4},{6,7},{7,6},{8,9},{9,8},{10,11... | collective-permute-start | bytes 1769480 | tf_op jit(solution)/shard_map/ppermute | solution.py:699
  91.5 19.7 %collective-permute-start.21 = (bf16[384,768]{1,0:T(8,128)(2,1)S(1)}, bf16[384,768]{1,0:T(8,128)(2,1)S(1)}, u32[]{:S(2)}, u32[]{:S(2)}) collective-permute-start(bf16[384,768]{1,0:T(8,128)(2,1)S(1)} %collective-permute-done.19.refs_3_.refs_9_), channel_id=1, source_target_pairs={{0,1},{1,0},{2,3},{3,2},{4,5},{5,4},{6,7},{7,6},{8,9},{9,8},{10,11... | collective-permute-start | bytes 1769480 | tf_op jit(solution)/shard_map/ppermute | solution.py:699
  182.7 94.1 %collective-permute-start.28 = (bf16[192,3072]{1,0:T(8,128)(2,1)}, bf16[192,3072]{1,0:T(8,128)(2,1)}, u32[]{:S(2)}, u32[]{:S(2)}) collective-permute-start(bf16[192,3072]{1,0:T(8,128)(2,1)} %fusion), channel_id=1, source_target_pairs={{0,2},{1,3},{2,0},{3,1},{4,6},{5,7},{6,4},{7,5},{8,10},{9,11},{10,... | collective-permute-start | bytes 3538952 | tf_op jit(solution)/shard_map/ppermute | solution.py:699
  187.0 93.5 %collective-permute-start.44 = (bf16[768,768]{1,0:T(8,128)(2,1)}, bf16[768,768]{1,0:T(8,128)(2,1)}, u32[]{:S(2)}, u32[]{:S(2)}) collective-permute-start(bf16[768,768]{1,0:T(8,128)(2,1)} %fusion.2), channel_id=1, source_target_pairs={{0,2},{1,3},{2,0},{3,1},{4,6},{5,7},{6,4},{7,5},{8,10},{9,11},{10,... | collective-permute-start | bytes 3538952 | tf_op jit(solution)/shard_map/ppermute | solution.py:699
  190.3 93.5 %collective-permute-start.36 = (bf16[192,3072]{1,0:T(8,128)(2,1)}, bf16[192,3072]{1,0:T(8,128)(2,1)S(1)}, u32[]{:S(2)}, u32[]{:S(2)}) collective-permute-start(bf16[192,3072]{1,0:T(8,128)(2,1)} %fusion.1), channel_id=1, source_target_pairs={{0,2},{1,3},{2,0},{3,1},{4,6},{5,7},{6,4},{7,5},{8,10},{9,11},{10,... | collective-permute-start | bytes 3538952 | tf_op jit(solution)/shard_map/ppermute | solution.py:699
  210.5 52.1 %collective-permute-start.23 = (f32[13,768]{1,0:T(8,128)S(1)}, f32[13,768]{1,0:T(8,128)S(1)}, u32[]{:S(2)}, u32[]{:S(2)}) collective-permute-start(f32[13,768]{1,0:T(8,128)S(1)} %add.218), channel_id=1, source_target_pairs={{0,2},{1,3},{2,0},{3,1},{4,6},{5,7},{6,4},{7,5},{8,10},{9,11},{10,... | collective-permute-start | bytes 119816 | tf_op jit(solution)/shard_map/ppermute | solution.py:699
  274.2 20.3 %collective-permute-start.26 = (f32[13,768]{1,0:T(8,128)}, f32[13,768]{1,0:T(8,128)}, u32[]{:S(2)}, u32[]{:S(2)}) collective-permute-start(f32[13,768]{1,0:T(8,128)} %add.221), channel_id=1, source_target_pairs={{0,16},{4,20},{8,24},{12,28},{16,0},{20,4},{24,8},{28,12},{1,17},{... | collective-permute-start | bytes 119816 | tf_op jit(solution)/shard_map/ppermute | solution.py:699
  282.2 26.7 %collective-permute-start.45 = (bf16[384,768]{1,0:T(8,128)(2,1)S(1)}, bf16[384,768]{1,0:T(8,128)(2,1)S(1)}, u32[]{:S(2)}, u32[]{:S(2)}) collective-permute-start(bf16[384,768]{1,0:T(8,128)(2,1)S(1)} %get-tuple-element.62), channel_id=1, source_target_pairs={{0,4},{4,0},{8,12},{12,8},{16,20},{20,16},{24,28},{28,24},{1,5},{5... | collective-permute-start | bytes 1769480 | tf_op jit(solution)/shard_map/ppermute | solution.py:699
  284.4 33.7 %collective-permute-start.37 = (bf16[96,3072]{1,0:T(8,128)(2,1)S(1)}, bf16[96,3072]{1,0:T(8,128)(2,1)S(1)}, u32[]{:S(2)}, u32[]{:S(2)}) collective-permute-start(bf16[96,3072]{1,0:T(8,128)(2,1)S(1)} %get-tuple-element.64), channel_id=1, source_target_pairs={{0,4},{4,0},{8,12},{12,8},{16,20},{20,16},{24,28},{28,24},{1,5},{5... | collective-permute-start | bytes 1769480 | tf_op jit(solution)/shard_map/ppermute | solution.py:699
  296.4 22.4 %collective-permute-start.30 = (bf16[48,3072]{1,0:T(8,128)(2,1)S(1)}, bf16[48,3072]{1,0:T(8,128)(2,1)S(1)}, u32[]{:S(2)}, u32[]{:S(2)}) collective-permute-start(bf16[48,3072]{1,0:T(8,128)(2,1)S(1)} %get-tuple-element.72), channel_id=1, source_target_pairs={{0,8},{4,12},{8,0},{12,4},{16,24},{20,28},{24,16},{28,20},{1,9},{5... | collective-permute-start | bytes 884744 | tf_op jit(solution)/shard_map/ppermute | solution.py:699
  319.3 19.6 %collective-permute-start.47 = (bf16[96,768]{1,0:T(8,128)(2,1)S(1)}, bf16[96,768]{1,0:T(8,128)(2,1)S(1)}, u32[]{:S(2)}, u32[]{:S(2)}) collective-permute-start(bf16[96,768]{1,0:T(8,128)(2,1)S(1)} %add_convert_fusion.10), channel_id=1, source_target_pairs={{0,16},{4,20},{8,24},{12,28},{16,0},{20,4},{24,8},{28,12},{1,17},{... | collective-permute-start | bytes 442376 | tf_op jit(solution)/shard_map/ppermute | solution.py:699
  329.3 20.7 %collective-permute-start.32 = (bf16[24,3072]{1,0:T(8,128)(2,1)S(1)}, bf16[24,3072]{1,0:T(8,128)(2,1)S(1)}, u32[]{:S(2)}, u32[]{:S(2)}) collective-permute-start(bf16[24,3072]{1,0:T(8,128)(2,1)S(1)} %add_convert_fusion.15), channel_id=1, source_target_pairs={{0,16},{4,20},{8,24},{12,28},{16,0},{20,4},{24,8},{28,12},{1,17},{... | collective-permute-start | bytes 442376 | tf_op jit(solution)/shard_map/ppermute | solution.py:699
  368.4 22.6 %collective-permute-start.50 = (bf16[384,768]{1,0:T(8,128)(2,1)S(1)}, bf16[384,768]{1,0:T(8,128)(2,1)S(1)}, u32[]{:S(2)}, u32[]{:S(2)}) collective-permute-start(bf16[384,768]{1,0:T(8,128)(2,1)S(1)} %maximum_select_fusion.5), channel_id=1, source_target_pairs={{0,4},{4,0},{8,12},{12,8},{16,20},{20,16},{24,28},{28,24},{1,5},{5... | collective-permute-start | bytes 1769480 | tf_op jit(solution)/shard_map/ppermute | solution.py:699
  374.2 27.6 %collective-permute-start.42 = (bf16[96,3072]{1,0:T(8,128)(2,1)S(1)}, bf16[96,3072]{1,0:T(8,128)(2,1)S(1)}, u32[]{:S(2)}, u32[]{:S(2)}) collective-permute-start(bf16[96,3072]{1,0:T(8,128)(2,1)S(1)} %maximum_select_fusion.4), channel_id=1, source_target_pairs={{0,4},{4,0},{8,12},{12,8},{16,20},{20,16},{24,28},{28,24},{1,5},{5... | collective-permute-start | bytes 1769480 | tf_op jit(solution)/shard_map/ppermute | solution.py:699
  (51 other events, 525.7 us)
